TPU v7x, 32 devices: a whole 2x2x4 slice. The times are simulated.
32 devices in a mesh: parts: 2 (over x), order: 8 (over z, y), lat: 2 (over core).
Axes of the slice: x: 2, y: 2, z: 4, core: 2. Of those that a mesh axis runs over, the one named last changes fastest.
Arguments:
- fourier: float32 [128, 16, 64, 128], P('parts', 'lat', 'order'), parts along dimension 0, may hold values from -6 to 6
- factors: float32 [64, 4, 16, 64, 128], P('order', None, 'lat'), may hold values from -0.5 to 0.5
- slot_of_order: int32 [64], replicated, may hold values from 0 to 63, each once
- ranks: int32 [64, 4], replicated, may hold values from 16 to 64
- pattern: int32 [64, 4, 16], replicated, may hold values 0 or 1
Outputs:
- spectra: float32 [128, 16, 64, 128], P(('parts', 'order'), 'lat'), parts along dimension 0
There are 2 independent parts, one for each index of `parts`. A program takes and returns all parts, laid end to end along the dimension named above; an argument that names none is the same for every part. Nothing has to cross between parts.
All inputs are finite; a program needn't handle non-finite values.
Results may differ from a plain program's by a relative error of at most 0.0003.
Values sent between devices are 32-bit elements; how exact they have to be, the bound alone decides.
No kernel may reach another device: no remote copies, remote signals or barrier semaphores. Data moves between devices by JAX's collectives and lax.ppermute only.
A program may use at most 64 MiB of HBM per device.

v0:
```python
import jax
import jax.numpy as jnp
from jax import lax
from jax.sharding import PartitionSpec as P

LEVELS = 4


def partner_2(block, axis, stride):
    count = lax.axis_size(axis)
    route = []
    for low in range(count):
        high = low | 1 << stride
        if high != low and high < count:
            route += [(low, high), (high, low)]
    return lax.ppermute(block, axis, route)


def per_device(fourier, factors, slot_of_order, ranks, pattern):
    slot_count = factors.shape[0]
    half_blocks = factors.shape[2]
    block_rows = factors.shape[3]
    columns = fourier.shape[3]
    groups = lax.axis_size("order")
    every_slot = jnp.arange(slot_count * groups, dtype=jnp.int32)
    hit_table = (slot_of_order[None, :] == every_slot[:, None]).astype(jnp.int32)
    packed = jnp.einsum(
        "so,obln->sbln", hit_table.astype(jnp.float32), fourier, precision=lax.Precision.HIGHEST
    )
    my_group = lax.axis_index("order")
    my_half = lax.axis_index("lat")
    my_hits = lax.dynamic_slice_in_dim(hit_table, my_group * slot_count, slot_count, 0)
    slot_rank = jnp.sum(my_hits[:, :, None] * ranks[None], axis=1)
    slot_pattern = jnp.sum(my_hits[:, :, None, None] * pattern[None], axis=1)
    slot_pattern = lax.dynamic_slice_in_dim(slot_pattern, my_half * half_blocks, half_blocks, 2)
    state = lax.all_to_all(packed, "order", split_axis=0, concat_axis=2, tiled=True)
    partner = partner_2(state, "lat", 0)
    lanes = jnp.arange(block_rows, dtype=jnp.int32)
    own_mask = jnp.ones((slot_count, half_blocks, block_rows), jnp.float32)
    for level in range(LEVELS):
        if level > 0:
            dist = half_blocks >> level
            folded = state.reshape(
                slot_count, half_blocks // (2 * dist), 2, dist, block_rows, columns
            )
            partner = jnp.flip(folded, axis=2).reshape(state.shape)
        keep = (lanes[None, :] < slot_rank[:, level][:, None]).astype(jnp.float32)
        pair_mask = keep[:, None, :] * slot_pattern[:, level][:, :, None].astype(jnp.float32)
        mask = jnp.concatenate([own_mask, pair_mask], axis=2)
        matrix = factors[:, level] * mask[:, :, None, :]
        stacked = jnp.concatenate([state, partner], axis=2)
        state = jnp.einsum("cbpq,cbqn->cbpn", matrix, stacked, precision=lax.Precision.HIGHEST)
    return state


def solution(mesh):
    return jax.shard_map(
        per_device,
        mesh=mesh,
        in_specs=(
            P("parts", "lat", "order", None),
            P("order", None, "lat", None, None),
            P(),
            P(),
            P(),
        ),
        out_specs=P(("parts", "order"), "lat", None, None),
        check_vma=False,
    )
```

profile of v0, /device:TPU:9, one launch (start us, length us, event | category | flops | bytes accessed | tf_op | source)
XLA Modules:
  0.0 107.8 jit_solution(12565620131098869125)
XLA Ops:
  0.0 0.0 copy-start
  0.0 1.6 %copy-done = f32[64,8,8,128]{3,2,1,0:T(8,128)S(1)} copy-done((f32[64,8,8,128]{3,2,1,0:T(8,128)S(1)}, f32[64,8,8,128]{3,2,1,0:T(8,128)}, u32[]{:S(2)}) %copy-start) | copy-done | bytes 2097176
  1.6 3.7 %fusion.16 = f32[64,8,8,128]{3,0,2,1:T(8,128)S(1)} fusion(f32[64,8,8,128]{3,2,1,0:T(8,128)S(1)} %copy-done, s32[64]{0:T(128)} %param.7), kind=kOutput, calls=%fused_computation.21 | convolution fusion | flops 402665472 | bytes 4194560 | tf_op jit(solution)/shard_map/so,obln->sbln/dot_general | solution.py:27
  5.3 1.2 %copy.16 = f32[64,8,8,128]{3,2,1,0:T(8,128)S(1)} copy(f32[64,8,8,128]{3,0,2,1:T(8,128)S(1)} %fusion.16) | data formatting | bytes 4194304 | tf_op jit(solution)/shard_map/so,obln->sbln/dot_general | solution.py:27
  6.5 51.9 %all_to_all.18 = f32[64,8,8,128]{3,2,1,0:T(8,128)S(1)} all-to-all(f32[64,8,8,128]{3,2,1,0:T(8,128)S(1)} %copy.16), channel_id=1, replica_groups=mesh['parts'=2,'order'=8,'lat'=2] {'order'}, dimensions={0} | all-to-all | bytes 4194304 | tf_op jit(solution)/shard_map/all_to_all | solution.py:36
  58.4 0.0 copy-start.2
  58.4 0.0 copy-start.3
  58.4 0.0 copy-start.1
  58.4 1.6 %copy.22 = f32[8,8,8,8,128]{4,3,0,2,1:T(8,128)} copy(f32[8,8,8,8,128]{4,3,2,1,0:T(8,128)S(1)} %bitcast.44) | data formatting | bytes 4194304 | tf_op jit(solution)/shard_map/all_to_all | solution.py:36
  60.1 2.2 %collective-permute-start = (f32[8,8,64,128]{3,2,1,0:T(8,128)}, f32[8,8,64,128]{3,2,1,0:T(8,128)}, u32[]{:S(2)}, u32[]{:S(2)}) collective-permute-start(f32[8,8,64,128]{3,2,1,0:T(8,128)} %bitcast.40), channel_id=1, source_target_pairs={{0,1},{1,0},{2,3},{3,2},{4,5},{5,4},{6,7},{7,6},{8,9},{9,8},{10,11... | collective-permute-start | bytes 6291464 | tf_op jit(solution)/shard_map/ppermute | solution.py:16
  62.2 0.0 copy-done.2
  62.2 0.0 copy-done.3
  62.3 0.1 multiply_reduce_fusion.1
  62.4 0.0 copy-done.1
  62.4 0.6 multiply_reduce_fusion
  63.0 0.1 dynamic-slice_convert_fusion.3
  63.2 0.1 fusion.32
  63.2 0.1 broadcast_multiply_fusion
  63.3 0.1 concatenate.27
  63.4 0.1 broadcast_multiply_fusion.1
  63.5 0.1 concatenate.26
  63.6 0.1 fusion.30
  63.6 0.1 broadcast_multiply_fusion.2
  63.7 0.1 concatenate.25
  63.8 0.1 broadcast_multiply_fusion.3
  63.9 0.1 concatenate.24
  64.0 2.4 %collective-permute-done = f32[8,8,64,128]{3,2,1,0:T(8,128)} collective-permute-done((f32[8,8,64,128]{3,2,1,0:T(8,128)}, f32[8,8,64,128]{3,2,1,0:T(8,128)}, u32[]{:S(2)}, u32[]{:S(2)}) %collective-permute-start) | collective-permute-done | bytes 2097184 | tf_op jit(solution)/shard_map/ppermute | solution.py:16
  66.3 8.0 %fusion = f32[8,8,64,128]{3,2,1,0:T(8,128)} fusion(f32[8,8,64,128]{3,2,1,0:T(8,128)} %collective-permute-done, f32[8,8,64,128]{3,2,1,0:T(8,128)} %bitcast.40, f32[8,4,8,64,128]{4,3,2,1,0:T(8,128)} %param.6, f32[8,8,128]{2,1,0:T(8,128)S(1)} %concatenate.27), kind=kOutput, calls=%fused_computation | convolution fusion | flops 806879232 | bytes 8421376 | tf_op jit(solution)/shard_map/cbpq,cbqn->cbpn/dot_general | solution.py:52
  74.3 3.2 %rev.12 = f32[8,1,2,4,64,128]{5,4,3,2,0,1:T(8,128)} reverse(f32[8,1,2,4,64,128]{5,4,3,2,0,1:T(8,128)} %bitcast.41), dimensions={2} | reverse | bytes 4194304 | tf_op jit(solution)/shard_map/jit(_flip)/rev | solution.py:46
  77.5 7.9 %fusion.4 = f32[8,8,64,128]{3,2,1,0:T(8,128)} fusion(f32[8,8,64,128]{3,2,1,0:T(8,128)} %bitcast.45, f32[8,8,64,128]{3,2,1,0:T(8,128)} %fusion, f32[8,4,8,64,128]{4,3,2,1,0:T(8,128)} %param.6, f32[8,8,128]{2,1,0:T(8,128)S(1)} %concatenate.26), kind=kOutput, calls=%fused_computation.4 | convolution fusion | flops 806879232 | bytes 8421376 | tf_op jit(solution)/shard_map/cbpq,cbqn->cbpn/dot_general | solution.py:52
  85.4 3.2 %rev.13 = f32[8,2,2,2,64,128]{5,4,3,2,1,0:T(8,128)} reverse(f32[8,2,2,2,64,128]{5,4,3,2,1,0:T(8,128)} %bitcast.42), dimensions={2} | reverse | bytes 4194304 | tf_op jit(solution)/shard_map/jit(_flip)/rev | solution.py:46
  88.6 8.2 %fusion.8 = f32[8,8,64,128]{3,2,1,0:T(8,128)} fusion(f32[8,8,64,128]{3,2,1,0:T(8,128)} %bitcast.46, f32[8,8,64,128]{3,2,1,0:T(8,128)} %fusion.4, f32[8,4,8,64,128]{4,3,2,1,0:T(8,128)} %param.6, f32[8,8,128]{2,1,0:T(8,128)S(1)} %concatenate.25), kind=kOutput, calls=%fused_computation.8 | convolution fusion | flops 806879232 | bytes 8421376 | tf_op jit(solution)/shard_map/cbpq,cbqn->cbpn/dot_general | solution.py:52
  96.7 3.1 %rev.14 = f32[8,4,2,1,64,128]{5,4,2,1,0,3:T(8,128)} reverse(f32[8,4,2,1,64,128]{5,4,2,1,0,3:T(8,128)} %bitcast.43), dimensions={2} | reverse | bytes 4194304 | tf_op jit(solution)/shard_map/jit(_flip)/rev | solution.py:46
  99.9 7.9 %fusion.12 = f32[8,8,64,128]{3,2,1,0:T(8,128)} fusion(f32[8,8,64,128]{3,2,1,0:T(8,128)} %bitcast.47, f32[8,8,64,128]{3,2,1,0:T(8,128)} %fusion.8, f32[8,4,8,64,128]{4,3,2,1,0:T(8,128)} %param.6, f32[8,8,128]{2,1,0:T(8,128)S(1)} %concatenate.24), kind=kOutput, calls=%fused_computation.12 | convolution fusion | flops 806879232 | bytes 8421376 | tf_op jit(solution)/shard_map/cbpq,cbqn->cbpn/dot_general | solution.py:52
  (3 shorter events, 0.0 us)
Async XLA Ops:
  0.0 1.6 %copy-start = (f32[64,8,8,128]{3,2,1,0:T(8,128)S(1)}, f32[64,8,8,128]{3,2,1,0:T(8,128)}, u32[]{:S(2)}) copy-start(f32[64,8,8,128]{3,2,1,0:T(8,128)} %param.5) | copy-start | bytes 6291460
  58.4 3.8 %copy-start.2 = (s32[64]{0:T(128)S(1)}, s32[64]{0:T(128)}, u32[]{:S(2)}) copy-start(s32[64]{0:T(128)} %param.7) | copy-start | bytes 772
  58.4 3.8 %copy-start.3 = (s32[64,4]{0,1:T(4,128)S(1)}, s32[64,4]{0,1:T(4,128)}, u32[]{:S(2)}) copy-start(s32[64,4]{0,1:T(4,128)} %param.8) | copy-start | bytes 3076
  58.4 4.0 %copy-start.1 = (s32[64,4,16]{0,2,1:T(8,128)S(1)}, s32[64,4,16]{0,2,1:T(8,128)}, u32[]{:S(2)}) copy-start(s32[64,4,16]{0,2,1:T(8,128)} %param.9) | copy-start | bytes 49156
  60.1 6.3 %collective-permute-start = (f32[8,8,64,128]{3,2,1,0:T(8,128)}, f32[8,8,64,128]{3,2,1,0:T(8,128)}, u32[]{:S(2)}, u32[]{:S(2)}) collective-permute-start(f32[8,8,64,128]{3,2,1,0:T(8,128)} %bitcast.40), channel_id=1, source_target_pairs={{0,1},{1,0},{2,3},{3,2},{4,5},{5,4},{6,7},{7,6},{8,9},{9,8},{10,11... | collective-permute-start | bytes 6291464 | tf_op jit(solution)/shard_map/ppermute | solution.py:16
where the time goes:
time: 110 us; the launch traced here: 108 us
  blocking collectives  51.9 us (47%)
  matrix products  35.7 us (32%)
  local copies, waits for them, and re-layouts  14.2 us (13%)
  waiting for transfers between devices  2.39 us (2%)
  starting transfers between devices  2.16 us (2%)
  other arithmetic  1.33 us (1%)
    all_to_all x1, blocking collectives, per_device(): lax.all_to_all(packed, 'order', split_axis=0, concat_axis=2, tiled=True)  51.9 us
    dot_general x4, matrix products, per_device(): jnp.einsum('cbpq,cbqn->cbpn', matrix, stacked, precision=lax.Precision.HI...  32 us
    rev x3, local copies, waits for them, and re-layouts, per_device(): partner = jnp.flip(folded, axis=2).reshape(state.shape)  9.46 us
    dot_general x1, matrix products, per_device(): jnp.einsum('so,obln->sbln', hit_table.astype(jnp.float32), fourier, preci...  3.69 us
    ppermute x1, waiting for transfers between devices, partner_2(): return lax.ppermute(block, axis, route)  2.39 us
  transfers between devices with their start and end apart: 1, of which 1 were waited for; matrix products, arithmetic and copies ran while one was open for 2% of the time, Pallas kernels for 0%

commit v1 on v0

v1 whole, which is shorter than its diff:
```python
import functools

import jax
import jax.numpy as jnp
from jax import lax
from jax.experimental import pallas as pl
from jax.experimental.pallas import tpu as pltpu
from jax.sharding import PartitionSpec as P

LEVELS = 4
CHUNKS = (6, 2)
ANY = pl.BlockSpec(memory_space=pl.ANY)
SMEM = pl.BlockSpec(memory_space=pltpu.SMEM)
VMEM = pl.BlockSpec(memory_space=pltpu.VMEM)


def in_vmem(x):
    return pltpu.with_memory_space_constraint(x, pltpu.VMEM)


def in_hbm(x):
    return pltpu.with_memory_space_constraint(x, pltpu.HBM)


def gather_kernel(plan, slot_count, n_after, slot_ref, rows_ref, *refs):
    refs = refs[n_after:]
    outs, (inverse, sems) = refs[: len(plan)], refs[len(plan) :]
    me = lax.axis_index("order")

    def invert(m, carry):
        inverse[slot_ref[m]] = m
        return carry

    lax.fori_loop(0, slot_ref.shape[0], invert, 0)
    for o, (hop, first, count) in enumerate(plan):
        base = (me ^ hop) * slot_count + first

        def issue(t, carry, o=o, base=base):
            pltpu.make_async_copy(
                rows_ref.at[inverse[base + t]], outs[o].at[t], sems.at[o]
            ).start()
            return carry

        lax.fori_loop(0, count, issue, 0, unroll=True)
    for o in range(len(plan)):
        pltpu.make_async_copy(outs[o], outs[o], sems.at[o]).wait()


def gather(plan, slot_count, slot_of_order, fourier, after=()):
    shapes = [pltpu.VMEM((count,) + fourier.shape[1:], fourier.dtype) for _, _, count in plan]
    size = sum(count for _, _, count in plan) * fourier[0].size * 4
    return pl.pallas_call(
        functools.partial(gather_kernel, plan, slot_count, len(after)),
        out_shape=shapes,
        in_specs=[SMEM, ANY] + [ANY] * len(after),
        out_specs=[VMEM] * len(plan),
        scratch_shapes=[
            pltpu.SMEM((slot_of_order.shape[0],), jnp.int32),
            pltpu.SemaphoreType.DMA((len(plan),)),
        ],
        compiler_params=pltpu.CompilerParams(vmem_limit_bytes=4 * 1024 * 1024),
        cost_estimate=pl.CostEstimate(flops=0, bytes_accessed=2 * size, transcendentals=0),
        name="gather_rows",
    )(slot_of_order, in_hbm(fourier), *after)


def join_kernel(plan, count, *refs):
    pieces, out = refs[: len(plan)], refs[len(plan)]
    me = lax.axis_index("order")
    for piece, (hop, first) in zip(pieces, plan):
        rows = piece.shape[2]
        low = pl.multiple_of((me ^ hop) * rows, rows)
        out[:, :, pl.ds(low, rows), :] = piece[first : first + count]


def join(plan, count, pieces):
    _, blocks, rows, columns = pieces[0].shape
    shape = (count, blocks, rows * len(plan), columns)
    size = 4 * count * blocks * rows * len(plan) * columns
    return pl.pallas_call(
        functools.partial(join_kernel, plan, count),
        out_shape=pltpu.VMEM(shape, pieces[0].dtype),
        in_specs=[VMEM] * len(plan),
        out_specs=VMEM,
        compiler_params=pltpu.CompilerParams(vmem_limit_bytes=4 * 1024 * 1024),
        cost_estimate=pl.CostEstimate(flops=0, bytes_accessed=2 * size, transcendentals=0),
        name="join_rows",
    )(*[in_vmem(piece) for piece in pieces])


def halves(x):
    high = x.astype(jnp.bfloat16)
    return high, (x - high.astype(jnp.float32)).astype(jnp.bfloat16)


def product(matrix, stacked):
    n = stacked.shape[1]
    high, low = halves(stacked)
    wide = jnp.concatenate([high, low], axis=1)
    wide = jnp.concatenate([wide, wide], axis=0)
    out = jnp.dot(
        jnp.concatenate(halves(matrix), axis=1), wide, preferred_element_type=jnp.float32
    )
    return out[:, :n] + out[:, n:]


def butterfly_kernel(first, bound_ref, factor_ref, own_ref, partner_ref, *refs):
    out_ref = refs[-1]
    _, levels, blocks, rows, width = factor_ref.shape
    here = pl.program_id(0)
    slot = here + first
    lanes = lax.broadcasted_iota(jnp.int32, (rows, width), 1)

    def matrix(level, i):
        keep = lanes < bound_ref[(slot * levels + level) * blocks + i]
        return jnp.where(keep, factor_ref[0, level, i], 0.0)

    state = []
    for i in range(blocks):
        stacked = jnp.concatenate([own_ref[here, i], partner_ref[here, i]], axis=0)
        state.append(product(matrix(0, i), stacked))
    for level in range(1, levels):
        dist = blocks >> level
        new = [None] * blocks
        for i in range(blocks):
            j = i ^ dist
            if j < i:
                continue
            stacked = jnp.concatenate([state[i], state[j]], axis=0)
            other = pltpu.roll(matrix(level, j), rows, 1)
            both = product(jnp.concatenate([matrix(level, i), other], axis=0), stacked)
            new[i], new[j] = both[:rows], both[rows:]
        state = new
    for i in range(blocks):
        out_ref[0, i] = state[i]


def butterfly(first, bound, factors, own, partner, so_far):
    count, blocks, rows, columns = own.shape
    slot_count, levels = factors.shape[:2]
    width = factors.shape[4]
    in_specs = [
        SMEM,
        pl.BlockSpec((1, levels, blocks, rows, width), lambda s: (s + first, 0, 0, 0, 0)),
        VMEM,
        VMEM,
    ]
    args = [bound, in_hbm(factors), in_vmem(own), in_vmem(partner)]
    if so_far is not None:
        in_specs.append(ANY)
        args.append(so_far)
    return pl.pallas_call(
        functools.partial(butterfly_kernel, first),
        grid=(count,),
        out_shape=jax.ShapeDtypeStruct((slot_count, blocks, rows, columns), own.dtype),
        in_specs=in_specs,
        out_specs=pl.BlockSpec((1, blocks, rows, columns), lambda s: (s + first, 0, 0, 0)),
        input_output_aliases={} if so_far is None else {4: 0},
        compiler_params=pltpu.CompilerParams(vmem_limit_bytes=16 * 1024 * 1024),
        cost_estimate=pl.CostEstimate(
            flops=count * levels * blocks * rows * width * columns * 8,
            bytes_accessed=4 * count * blocks * rows * (levels * width + 3 * columns),
            transcendentals=0,
        ),
        name="butterfly",
    )(*args)


def coupling_bounds(slot_of_order, ranks, pattern, slot_count, blocks, rows):
    my_slots = lax.axis_index("order") * slot_count + jnp.arange(slot_count, dtype=jnp.int32)
    hits = (slot_of_order[None, :] == my_slots[:, None]).astype(jnp.int32)
    slot_rank = jnp.sum(hits[:, :, None] * ranks[None], axis=1)
    mine = lax.dynamic_slice_in_dim(pattern, lax.axis_index("lat") * blocks, blocks, 2)
    slot_pattern = jnp.sum(hits[:, :, None, None] * mine[None], axis=1)
    return (rows + slot_pattern * slot_rank[:, :, None]).reshape(-1)


def per_device(fourier, factors, slot_of_order, ranks, pattern):
    slot_count, _, blocks, block_rows, _ = factors.shape
    rows = fourier.shape[2]
    groups = lax.axis_size("order")
    bound = coupling_bounds(slot_of_order, ranks, pattern, slot_count, blocks, block_rows)
    swap = [(0, 1), (1, 0)]

    if rows % 8 or groups > 8 or groups & (groups - 1) or sum(CHUNKS) != slot_count:
        (packed,) = gather(((0, 0, slot_of_order.shape[0]),), 0, slot_of_order, fourier)
        own = lax.all_to_all(packed, "order", split_axis=0, concat_axis=2, tiled=True)
        return butterfly(0, bound, factors, own, lax.ppermute(own, "lat", swap), None)

    def hop(piece, k):
        return lax.ppermute(piece, "order", [(g, g ^ k) for g in range(groups)])

    near = list(range(1, groups // 2))
    far = list(range(groups // 2, groups))
    firsts = [sum(CHUNKS[:c]) for c in range(len(CHUNKS))]
    sent = gather([(k, 0, CHUNKS[0]) for k in far], slot_count, slot_of_order, fourier)
    far_pieces = [[hop(piece, k) for piece, k in zip(sent, far)]]
    plan = [(k, 0, slot_count) for k in [0] + near]
    for first, count in zip(firsts[1:], CHUNKS[1:]):
        plan += [(k, first, count) for k in far]
    sent = gather(plan, slot_count, slot_of_order, fourier)
    near_pieces = [sent[0]] + [hop(piece, k) for piece, k in zip(sent[1:], near)]
    rest = sent[len(near_pieces) :]
    for c in range(1, len(CHUNKS)):
        far_pieces.append([hop(piece, k) for piece, k in zip(rest, far)])
        rest = rest[len(far) :]
    out = None
    for first, count, pieces in zip(firsts, CHUNKS, far_pieces):
        plan = [(k, first) for k in [0] + near] + [(k, 0) for k in far]
        own = join(plan, count, near_pieces + pieces)
        out = butterfly(first, bound, factors, own, lax.ppermute(own, "lat", swap), out)
    return out


def solution(mesh):
    return jax.shard_map(
        per_device,
        mesh=mesh,
        in_specs=(
            P("parts", "lat", "order", None),
            P("order", None, "lat", None, None),
            P(),
            P(),
            P(),
        ),
        out_specs=P(("parts", "order"), "lat", None, None),
        check_vma=False,
    )
```

time: 110 us -> 71.9 us (0.65)
  blocking collectives: 51.9 us -> 0 us
  matrix products: 35.7 us -> 0 us
  waiting for transfers between devices: 2.39 us -> 36.5 us
  Pallas kernels: 0 us -> 18.3 us
  local copies, waits for them, and re-layouts: 14.2 us -> 0.87 us
  starting transfers between devices: 2.16 us -> 14.1 us
    all_to_all x1 -> x0, blocking collectives: 51.9 us -> none  [per_device(): lax.all_to_all(packed, 'order', split_axis=0, concat_axis=2, tiled=True)]
    dot_general x5 -> x0, matrix products: 35.7 us -> none  [the longest x4 32 us: per_device(): jnp.einsum('cbpq,cbqn->cbpn', matrix, stacked, precision=lax.Precision.HI...]
    ppermute x1 -> x13, waiting for transfers between devices: 2.39 us -> 36.5 us  [the longest x11 36.5 us: hop(): return lax.ppermute(piece, 'order', [(g, g ^ k) for g in range(groups)])]
    pallas_call x0 -> x6, Pallas kernels: none -> 18.3 us  [the longest x2 12.7 us: butterfly(): pl.pallas_call(functools.partial(butterfly_kernel, first), grid=(count,),...]
    ppermute x1 -> x13, starting transfers between devices: 2.16 us -> 14.1 us  [the longest x11 11.9 us: hop(): return lax.ppermute(piece, 'order', [(g, g ^ k) for g in range(groups)])]
    rev x3 -> x0, local copies, waits for them, and re-layouts: 9.46 us -> none  [per_device(): partner = jnp.flip(folded, axis=2).reshape(state.shape)]
    all_to_all x1 -> x0, local copies, waits for them, and re-layouts: 1.6 us -> none  [per_device(): lax.all_to_all(packed, 'order', split_axis=0, concat_axis=2, tiled=True)]
    dot_general x1 -> x0, local copies, waits for them, and re-layouts: 1.22 us -> none  [per_device(): jnp.einsum('so,obln->sbln', hit_table.astype(jnp.float32), fourier, preci...]
  transfers between devices with their start and end apart: 1 -> 13, of which waited for: 1 -> 8; matrix products, arithmetic and copies ran while one was open for 2% -> 2% of each run, Pallas kernels for 0% -> 17%
where the time goes in v1:
time: 71.9 us; the launch traced here: 70.8 us
  waiting for transfers between devices  36.5 us (51%)
  Pallas kernels  18.3 us (25%)
  starting transfers between devices  14.1 us (20%)
  other arithmetic  0.93 us (1%)
  local copies, waits for them, and re-layouts  0.87 us (1%)
    ppermute x11, waiting for transfers between devices, hop(): return lax.ppermute(piece, 'order', [(g, g ^ k) for g in range(groups)])  36.5 us
    pallas_call x2, Pallas kernels, butterfly(): pl.pallas_call(functools.partial(butterfly_kernel, first), grid=(count,),...  12.7 us
    ppermute x11, starting transfers between devices, hop(): return lax.ppermute(piece, 'order', [(g, g ^ k) for g in range(groups)])  11.9 us
    pallas_call x2, Pallas kernels, gather(): pl.pallas_call(functools.partial(gather_kernel, plan, slot_count, len(aft...  5.39 us
    ppermute x2, starting transfers between devices, per_device(): lax.ppermute(own, 'lat', swap)  2.2 us
  transfers between devices with their start and end apart: 13, of which 8 were waited for; matrix products, arithmetic and copies ran while one was open for 2% of the time, Pallas kernels for 17%

profile of v1, /device:TPU:9, one launch (start us, length us, event | category | flops | bytes accessed | tf_op | source)
XLA Modules:
  0.0 70.8 jit_solution(5644236234595464885)
XLA Ops:
  0.0 0.0 copy-start
  0.0 0.0 copy-start.1
  0.0 0.7 copy-done.1
  0.7 2.3 %gather_rows.3 = (f32[6,8,8,128]{3,2,1,0:T(8,128)S(1)}, f32[6,8,8,128]{3,2,1,0:T(8,128)S(1)}, f32[6,8,8,128]{3,2,1,0:T(8,128)S(1)}, f32[6,8,8,128]{3,2,1,0:T(8,128)S(1)}) custom-call(s32[64]{0:T(128)S(1)} %copy-done.1, f32[64,8,8,128]{3,2,1,0:T(8,128)} %rows_ref.3), custom_call_target="tpu_custom_call" | custom-call | bytes 1572864 | tf_op jit(solution)/shard_map/gather_rows/pallas_call | solution.py:52
  3.0 2.4 %collective-permute-start.8 = (f32[6,8,8,128]{3,2,1,0:T(8,128)S(1)}, f32[6,8,8,128]{3,2,1,0:T(8,128)S(1)}, u32[]{:S(2)}, u32[]{:S(2)}) collective-permute-start(f32[6,8,8,128]{3,2,1,0:T(8,128)S(1)} %get-tuple-element.25), channel_id=1, source_target_pairs={{0,8},{2,10},{4,12},{6,14},{8,0},{10,2},{12,4},{14,6},{1,9},{3,11}... | collective-permute-start | bytes 589832 | tf_op jit(solution)/shard_map/ppermute | solution.py:191
  5.3 1.0 %collective-permute-start.9 = (f32[6,8,8,128]{3,2,1,0:T(8,128)S(1)}, f32[6,8,8,128]{3,2,1,0:T(8,128)S(1)}, u32[]{:S(2)}, u32[]{:S(2)}) collective-permute-start(f32[6,8,8,128]{3,2,1,0:T(8,128)S(1)} %get-tuple-element.26), channel_id=1, source_target_pairs={{0,10},{2,8},{4,14},{6,12},{8,2},{10,0},{12,6},{14,4},{1,11},{3,9}... | collective-permute-start | bytes 589832 | tf_op jit(solution)/shard_map/ppermute | solution.py:191
  6.4 3.1 %gather_rows.2 = (f32[8,8,8,128]{3,2,1,0:T(8,128)S(1)}, f32[8,8,8,128]{3,2,1,0:T(8,128)S(1)}, f32[8,8,8,128]{3,2,1,0:T(8,128)S(1)}, f32[8,8,8,128]{3,2,1,0:T(8,1...) custom-call(s32[64]{0:T(128)S(1)} %copy-done.1, ...), custom_call_target="tpu_custom_call" | custom-call | bytes 2621440 | tf_op jit(solution)/shard_map/gather_rows/pallas_call | solution.py:52
  9.5 0.0 copy-start.2
  9.5 0.3 collective-permute-start
  9.8 0.2 collective-permute-start.1
  10.0 2.3 %collective-permute-start.2 = (f32[8,8,8,128]{3,2,1,0:T(8,128)S(1)}, f32[8,8,8,128]{3,2,1,0:T(8,128)S(1)}, u32[]{:S(2)}, u32[]{:S(2)}) collective-permute-start(f32[8,8,8,128]{3,2,1,0:T(8,128)S(1)} %get-tuple-element.20), channel_id=1, source_target_pairs={{0,6},{2,4},{4,2},{6,0},{8,14},{10,12},{12,10},{14,8},{1,7},{3,5},... | collective-permute-start | bytes 786440 | tf_op jit(solution)/shard_map/ppermute | solution.py:191
  12.2 6.1 %collective-permute-done.8.refs_4_ = f32[6,8,8,128]{3,2,1,0:T(8,128)S(1)} collective-permute-done((f32[6,8,8,128]{3,2,1,0:T(8,128)S(1)}, f32[6,8,8,128]{3,2,1,0:T(8,128)S(1)}, u32[]{:S(2)}, u32[]{:S(2)}) %collective-permute-start.8) | collective-permute-done | bytes 196640 | tf_op jit(solution)/shard_map/ppermute | solution.py:191
  18.3 0.0 collective-permute-start.10
  18.3 4.2 %collective-permute-done.9.refs_5_ = f32[6,8,8,128]{3,2,1,0:T(8,128)S(1)} collective-permute-done((f32[6,8,8,128]{3,2,1,0:T(8,128)S(1)}, f32[6,8,8,128]{3,2,1,0:T(8,128)S(1)}, u32[]{:S(2)}, u32[]{:S(2)}) %collective-permute-start.9) | collective-permute-done | bytes 196640 | tf_op jit(solution)/shard_map/ppermute | solution.py:191
  22.5 0.0 collective-permute-start.11
  22.5 12.6 %collective-permute-done.10.refs_6_ = f32[6,8,8,128]{3,2,1,0:T(8,128)S(1)} collective-permute-done((f32[6,8,8,128]{3,2,1,0:T(8,128)S(1)}, f32[6,8,8,128]{3,2,1,0:T(8,128)S(1)}, u32[]{:S(2)}, u32[]{:S(2)}) %collective-permute-start.10) | collective-permute-done | bytes 196640 | tf_op jit(solution)/shard_map/ppermute | solution.py:191
  35.2 4.2 %collective-permute-done.11.refs_7_ = f32[6,8,8,128]{3,2,1,0:T(8,128)S(1)} collective-permute-done((f32[6,8,8,128]{3,2,1,0:T(8,128)S(1)}, f32[6,8,8,128]{3,2,1,0:T(8,128)S(1)}, u32[]{:S(2)}, u32[]{:S(2)}) %collective-permute-start.11) | collective-permute-done | bytes 196640 | tf_op jit(solution)/shard_map/ppermute | solution.py:191
  39.4 0.0 collective-permute-done.refs_1_
  39.4 0.0 collective-permute-done.1.refs_2_
  39.4 0.0 collective-permute-done.2.refs_3_
  39.4 0.0 copy-start.3
  39.4 0.2 join_rows.3.own_ref
  39.6 1.4 %collective-permute-start.12 = (f32[6,8,64,128]{3,2,1,0:T(8,128)S(1)}, f32[6,8,64,128]{3,2,1,0:T(8,128)}, u32[]{:S(2)}, u32[]{:S(2)}) collective-permute-start(f32[6,8,64,128]{3,2,1,0:T(8,128)S(1)} %join_rows.3.own_ref), channel_id=1, source_target_pairs={{0,1},{1,0},{2,3},{3,2},{4,5},{5,4},{6,7},{7,6},{8,9},{9,8},{10,11... | collective-permute-start | bytes 4718600 | tf_op jit(solution)/shard_map/ppermute | solution.py:211
  41.0 3.4 %collective-permute-start.3 = (f32[2,8,8,128]{3,2,1,0:T(8,128)}, f32[2,8,8,128]{3,2,1,0:T(8,128)S(1)}, u32[]{:S(2)}, u32[]{:S(2)}) collective-permute-start(f32[2,8,8,128]{3,2,1,0:T(8,128)} %get-tuple-element.21), channel_id=1, source_target_pairs={{0,8},{2,10},{4,12},{6,14},{8,0},{10,2},{12,4},{14,6},{1,9},{3,11}... | collective-permute-start | bytes 196616 | tf_op jit(solution)/shard_map/ppermute | solution.py:191
  44.4 0.0 collective-permute-start.4
  44.4 1.2 %collective-permute-start.5 = (f32[2,8,8,128]{3,2,1,0:T(8,128)S(1)}, f32[2,8,8,128]{3,2,1,0:T(8,128)S(1)}, u32[]{:S(2)}, u32[]{:S(2)}) collective-permute-start(f32[2,8,8,128]{3,2,1,0:T(8,128)S(1)} %get-tuple-element.23), channel_id=1, source_target_pairs={{0,12},{2,14},{4,8},{6,10},{8,4},{10,6},{12,0},{14,2},{1,13},{3,15... | collective-permute-start | bytes 196616 | tf_op jit(solution)/shard_map/ppermute | solution.py:191
  45.6 1.1 %collective-permute-start.6 = (f32[2,8,8,128]{3,2,1,0:T(8,128)S(1)}, f32[2,8,8,128]{3,2,1,0:T(8,128)S(1)}, u32[]{:S(2)}, u32[]{:S(2)}) collective-permute-start(f32[2,8,8,128]{3,2,1,0:T(8,128)S(1)} %get-tuple-element.24), channel_id=1, source_target_pairs={{0,14},{2,12},{4,10},{6,8},{8,6},{10,4},{12,2},{14,0},{1,15},{3,13... | collective-permute-start | bytes 196616 | tf_op jit(solution)/shard_map/ppermute | solution.py:191
  46.8 0.0 copy-done.2
  46.8 0.1 compare_convert_fusion
  46.8 0.0 copy-done
  46.8 5.0 %collective-permute-done.3.refs_4_ = f32[2,8,8,128]{3,2,1,0:T(8,128)S(1)} collective-permute-done((f32[2,8,8,128]{3,2,1,0:T(8,128)}, f32[2,8,8,128]{3,2,1,0:T(8,128)S(1)}, u32[]{:S(2)}, u32[]{:S(2)}) %collective-permute-start.3) | collective-permute-done | bytes 65568 | tf_op jit(solution)/shard_map/ppermute | solution.py:191
  51.9 1.5 %collective-permute-done.4.refs_5_ = f32[2,8,8,128]{3,2,1,0:T(8,128)S(1)} collective-permute-done((f32[2,8,8,128]{3,2,1,0:T(8,128)}, f32[2,8,8,128]{3,2,1,0:T(8,128)S(1)}, u32[]{:S(2)}, u32[]{:S(2)}) %collective-permute-start.4) | collective-permute-done | bytes 65568 | tf_op jit(solution)/shard_map/ppermute | solution.py:191
  53.4 1.3 %collective-permute-done.5.refs_6_ = f32[2,8,8,128]{3,2,1,0:T(8,128)S(1)} collective-permute-done((f32[2,8,8,128]{3,2,1,0:T(8,128)S(1)}, f32[2,8,8,128]{3,2,1,0:T(8,128)S(1)}, u32[]{:S(2)}, u32[]{:S(2)}) %collective-permute-start.5) | collective-permute-done | bytes 65568 | tf_op jit(solution)/shard_map/ppermute | solution.py:191
  54.7 1.4 %collective-permute-done.6.refs_7_ = f32[2,8,8,128]{3,2,1,0:T(8,128)S(1)} collective-permute-done((f32[2,8,8,128]{3,2,1,0:T(8,128)S(1)}, f32[2,8,8,128]{3,2,1,0:T(8,128)S(1)}, u32[]{:S(2)}, u32[]{:S(2)}) %collective-permute-start.6) | collective-permute-done | bytes 65568 | tf_op jit(solution)/shard_map/ppermute | solution.py:191
  56.1 0.1 join_rows.2.own_ref
  56.2 0.8 %collective-permute-start.7 = (f32[2,8,64,128]{3,2,1,0:T(8,128)S(1)}, f32[2,8,64,128]{3,2,1,0:T(8,128)S(1)}, u32[]{:S(2)}, u32[]{:S(2)}) collective-permute-start(f32[2,8,64,128]{3,2,1,0:T(8,128)S(1)} %join_rows.2.own_ref), channel_id=1, source_target_pairs={{0,1},{1,0},{2,3},{3,2},{4,5},{5,4},{6,7},{7,6},{8,9},{9,8},{10,11... | collective-permute-start | bytes 1572872 | tf_op jit(solution)/shard_map/ppermute | solution.py:211
  57.0 0.0 copy-done.3
  57.0 0.1 multiply_reduce_fusion.1
  57.2 0.1 copy.9
  57.2 0.6 multiply_reduce_fusion
  57.9 0.1 multiply_add_fusion
  58.0 0.1 add.28.bound_ref
  58.1 0.0 collective-permute-done.12.partner_ref
  58.1 8.9 %butterfly.2.refs_0_ = f32[8,8,64,128]{3,2,1,0:T(8,128)} custom-call(s32[256]{0:T(256)S(1)} %add.28.bound_ref, f32[8,4,8,64,128]{4,3,2,1,0:T(8,128)} %factor_ref.3, f32[6,8,64,128]{3,2,1,0:T(8,128)S(1)} %join_rows.3.own_ref, f32[6,8,64,128]{3,2,1,0:T(8,128)} %collective-permute-done.12.partner_ref), custom_call_target="tpu_custom_call" | custom-call | flops 1610612736 | bytes 11010048 | tf_op jit(solution)/shard_map/butterfly/pallas_call | solution.py:152
  67.0 0.0 collective-permute-done.7.partner_ref
  67.0 3.8 %butterfly.3 = f32[8,8,64,128]{3,2,1,0:T(8,128)} custom-call(s32[256]{0:T(256)S(1)} %add.28.bound_ref, f32[8,4,8,64,128]{4,3,2,1,0:T(8,128)} %factor_ref.3, f32[2,8,64,128]{3,2,1,0:T(8,128)S(1)} %join_rows.2.own_ref, f32[2,8,64,128]{3,2,1,0:T(8,128)S(1)} %collective-permute-done.7.partner_ref, ...), custom_call_target="tpu_custom_call", output_to_operand_aliasing={{}: (4, {})} | custom-call | flops 536870912 | bytes 3670016 | tf_op jit(solution)/shard_map/butterfly/pallas_call | solution.py:152
  (2 shorter events, 0.0 us)
Async XLA Ops:
  0.0 46.8 %copy-start = (s32[64,4,16]{0,2,1:T(8,128)S(1)}, s32[64,4,16]{0,2,1:T(8,128)}, u32[]{:S(2)}) copy-start(s32[64,4,16]{0,2,1:T(8,128)} %param.9) | copy-start | bytes 49156
  0.0 0.7 copy-start.1
  3.0 15.4 %collective-permute-start.8 = (f32[6,8,8,128]{3,2,1,0:T(8,128)S(1)}, f32[6,8,8,128]{3,2,1,0:T(8,128)S(1)}, u32[]{:S(2)}, u32[]{:S(2)}) collective-permute-start(f32[6,8,8,128]{3,2,1,0:T(8,128)S(1)} %get-tuple-element.25), channel_id=1, source_target_pairs={{0,8},{2,10},{4,12},{6,14},{8,0},{10,2},{12,4},{14,6},{1,9},{3,11}... | collective-permute-start | bytes 589832 | tf_op jit(solution)/shard_map/ppermute | solution.py:191
  5.3 17.2 %collective-permute-start.9 = (f32[6,8,8,128]{3,2,1,0:T(8,128)S(1)}, f32[6,8,8,128]{3,2,1,0:T(8,128)S(1)}, u32[]{:S(2)}, u32[]{:S(2)}) collective-permute-start(f32[6,8,8,128]{3,2,1,0:T(8,128)S(1)} %get-tuple-element.26), channel_id=1, source_target_pairs={{0,10},{2,8},{4,14},{6,12},{8,2},{10,0},{12,6},{14,4},{1,11},{3,9}... | collective-permute-start | bytes 589832 | tf_op jit(solution)/shard_map/ppermute | solution.py:191
  9.5 37.3 %copy-start.2 = (s32[64]{0:T(128)S(1)}, s32[64]{0:T(128)}, u32[]{:S(2)}) copy-start(s32[64]{0:T(128)} %slot_ref.3) | copy-start | bytes 772
  9.5 29.9 %collective-permute-start = (f32[8,8,8,128]{3,2,1,0:T(8,128)S(1)}, f32[8,8,8,128]{3,2,1,0:T(8,128)S(1)}, u32[]{:S(2)}, u32[]{:S(2)}) collective-permute-start(f32[8,8,8,128]{3,2,1,0:T(8,128)S(1)} %get-tuple-element.18), channel_id=1, source_target_pairs={{0,2},{2,0},{4,6},{6,4},{8,10},{10,8},{12,14},{14,12},{1,3},{3,1},... | collective-permute-start | bytes 786440 | tf_op jit(solution)/shard_map/ppermute | solution.py:191
  9.8 29.6 %collective-permute-start.1 = (f32[8,8,8,128]{3,2,1,0:T(8,128)S(1)}, f32[8,8,8,128]{3,2,1,0:T(8,128)S(1)}, u32[]{:S(2)}, u32[]{:S(2)}) collective-permute-start(f32[8,8,8,128]{3,2,1,0:T(8,128)S(1)} %get-tuple-element.19), channel_id=1, source_target_pairs={{0,4},{2,6},{4,0},{6,2},{8,12},{10,14},{12,8},{14,10},{1,5},{3,7},... | collective-permute-start | bytes 786440 | tf_op jit(solution)/shard_map/ppermute | solution.py:191
  10.0 29.4 %collective-permute-start.2 = (f32[8,8,8,128]{3,2,1,0:T(8,128)S(1)}, f32[8,8,8,128]{3,2,1,0:T(8,128)S(1)}, u32[]{:S(2)}, u32[]{:S(2)}) collective-permute-start(f32[8,8,8,128]{3,2,1,0:T(8,128)S(1)} %get-tuple-element.20), channel_id=1, source_target_pairs={{0,6},{2,4},{4,2},{6,0},{8,14},{10,12},{12,10},{14,8},{1,7},{3,5},... | collective-permute-start | bytes 786440 | tf_op jit(solution)/shard_map/ppermute | solution.py:191
  18.3 16.9 %collective-permute-start.10 = (f32[6,8,8,128]{3,2,1,0:T(8,128)S(1)}, f32[6,8,8,128]{3,2,1,0:T(8,128)S(1)}, u32[]{:S(2)}, u32[]{:S(2)}) collective-permute-start(f32[6,8,8,128]{3,2,1,0:T(8,128)S(1)} %get-tuple-element.27), channel_id=1, source_target_pairs={{0,12},{2,14},{4,8},{6,10},{8,4},{10,6},{12,0},{14,2},{1,13},{3,15... | collective-permute-start | bytes 589832 | tf_op jit(solution)/shard_map/ppermute | solution.py:191
  22.5 16.9 %collective-permute-start.11 = (f32[6,8,8,128]{3,2,1,0:T(8,128)S(1)}, f32[6,8,8,128]{3,2,1,0:T(8,128)S(1)}, u32[]{:S(2)}, u32[]{:S(2)}) collective-permute-start(f32[6,8,8,128]{3,2,1,0:T(8,128)S(1)} %get-tuple-element.28), channel_id=1, source_target_pairs={{0,14},{2,12},{4,10},{6,8},{8,6},{10,4},{12,2},{14,0},{1,15},{3,13... | collective-permute-start | bytes 589832 | tf_op jit(solution)/shard_map/ppermute | solution.py:191
  39.4 17.6 %copy-start.3 = (s32[64,4]{0,1:T(4,128)S(1)}, s32[64,4]{0,1:T(4,128)}, u32[]{:S(2)}) copy-start(s32[64,4]{0,1:T(4,128)} %param.8) | copy-start | bytes 3076
  39.6 18.5 %collective-permute-start.12 = (f32[6,8,64,128]{3,2,1,0:T(8,128)S(1)}, f32[6,8,64,128]{3,2,1,0:T(8,128)}, u32[]{:S(2)}, u32[]{:S(2)}) collective-permute-start(f32[6,8,64,128]{3,2,1,0:T(8,128)S(1)} %join_rows.3.own_ref), channel_id=1, source_target_pairs={{0,1},{1,0},{2,3},{3,2},{4,5},{5,4},{6,7},{7,6},{8,9},{9,8},{10,11... | collective-permute-start | bytes 4718600 | tf_op jit(solution)/shard_map/ppermute | solution.py:211
  41.0 10.9 %collective-permute-start.3 = (f32[2,8,8,128]{3,2,1,0:T(8,128)}, f32[2,8,8,128]{3,2,1,0:T(8,128)S(1)}, u32[]{:S(2)}, u32[]{:S(2)}) collective-permute-start(f32[2,8,8,128]{3,2,1,0:T(8,128)} %get-tuple-element.21), channel_id=1, source_target_pairs={{0,8},{2,10},{4,12},{6,14},{8,0},{10,2},{12,4},{14,6},{1,9},{3,11}... | collective-permute-start | bytes 196616 | tf_op jit(solution)/shard_map/ppermute | solution.py:191
  44.4 9.0 %collective-permute-start.4 = (f32[2,8,8,128]{3,2,1,0:T(8,128)}, f32[2,8,8,128]{3,2,1,0:T(8,128)S(1)}, u32[]{:S(2)}, u32[]{:S(2)}) collective-permute-start(f32[2,8,8,128]{3,2,1,0:T(8,128)} %get-tuple-element.22), channel_id=1, source_target_pairs={{0,10},{2,8},{4,14},{6,12},{8,2},{10,0},{12,6},{14,4},{1,11},{3,9}... | collective-permute-start | bytes 196616 | tf_op jit(solution)/shard_map/ppermute | solution.py:191
  44.4 10.3 %collective-permute-start.5 = (f32[2,8,8,128]{3,2,1,0:T(8,128)S(1)}, f32[2,8,8,128]{3,2,1,0:T(8,128)S(1)}, u32[]{:S(2)}, u32[]{:S(2)}) collective-permute-start(f32[2,8,8,128]{3,2,1,0:T(8,128)S(1)} %get-tuple-element.23), channel_id=1, source_target_pairs={{0,12},{2,14},{4,8},{6,10},{8,4},{10,6},{12,0},{14,2},{1,13},{3,15... | collective-permute-start | bytes 196616 | tf_op jit(solution)/shard_map/ppermute | solution.py:191
  45.6 10.5 %collective-permute-start.6 = (f32[2,8,8,128]{3,2,1,0:T(8,128)S(1)}, f32[2,8,8,128]{3,2,1,0:T(8,128)S(1)}, u32[]{:S(2)}, u32[]{:S(2)}) collective-permute-start(f32[2,8,8,128]{3,2,1,0:T(8,128)S(1)} %get-tuple-element.24), channel_id=1, source_target_pairs={{0,14},{2,12},{4,10},{6,8},{8,6},{10,4},{12,2},{14,0},{1,15},{3,13... | collective-permute-start | bytes 196616 | tf_op jit(solution)/shard_map/ppermute | solution.py:191
  56.2 10.8 %collective-permute-start.7 = (f32[2,8,64,128]{3,2,1,0:T(8,128)S(1)}, f32[2,8,64,128]{3,2,1,0:T(8,128)S(1)}, u32[]{:S(2)}, u32[]{:S(2)}) collective-permute-start(f32[2,8,64,128]{3,2,1,0:T(8,128)S(1)} %join_rows.2.own_ref), channel_id=1, source_target_pairs={{0,1},{1,0},{2,3},{3,2},{4,5},{5,4},{6,7},{7,6},{8,9},{9,8},{10,11... | collective-permute-start | bytes 1572872 | tf_op jit(solution)/shard_map/ppermute | solution.py:211

commit v2 on v1

v2 whole, which is shorter than its diff:
```python
import functools

import jax
import jax.numpy as jnp
from jax import lax
from jax.experimental import pallas as pl
from jax.experimental.pallas import tpu as pltpu
from jax.sharding import PartitionSpec as P

LEVELS = 4
CHUNKS = ((0, 6), (6, 2))
FAR = ((0, 0, 6, 0, None), (1, 0, 6, 0, None), (2, 0, 6, 0, 0), (3, 0, 6, 0, 1), (0, 6, 2, 1, 2), (1, 6, 2, 1, 3), (2, 6, 2, 1, -1), (3, 6, 2, 1, -1))
TOGETHER = 3
EARLY = None
US = 10**9
COUPLE_FLOPS = 30 * US
BUTTERFLY_FLOPS = 0
JOIN_FLOPS = 30 * US
ANY = pl.BlockSpec(memory_space=pl.ANY)
SMEM = pl.BlockSpec(memory_space=pltpu.SMEM)
VMEM = pl.BlockSpec(memory_space=pltpu.VMEM)


def in_vmem(x):
    return pltpu.with_memory_space_constraint(x, pltpu.VMEM)


def in_hbm(x):
    return pltpu.with_memory_space_constraint(x, pltpu.HBM)


def gather_kernel(plan, slot_count, n_after, slot_ref, rows_ref, *refs):
    refs = refs[n_after:]
    outs, (slots, inverse, load_sem, sems) = refs[: len(plan)], refs[len(plan) :]
    me = lax.axis_index("order")
    load = pltpu.make_async_copy(slot_ref, slots, load_sem)
    load.start()
    load.wait()

    def invert(m, carry):
        inverse[slots[m]] = m
        return carry

    lax.fori_loop(0, slots.shape[0], invert, 0, unroll=16)
    for o, (hop, first, count) in enumerate(plan):
        base = (me ^ hop) * slot_count + first

        def issue(t, carry, o=o, base=base):
            pltpu.make_async_copy(
                rows_ref.at[inverse[base + t]], outs[o].at[t], sems.at[o]
            ).start()
            return carry

        lax.fori_loop(0, count, issue, 0, unroll=True)
    for o in range(len(plan)):
        pltpu.make_async_copy(outs[o], outs[o], sems.at[o]).wait()


def gather(plan, slot_count, slot_of_order, fourier, after=()):
    shapes = [pltpu.VMEM((count,) + fourier.shape[1:], fourier.dtype) for _, _, count in plan]
    size = sum(count for _, _, count in plan) * fourier[0].size * 4
    return pl.pallas_call(
        functools.partial(gather_kernel, plan, slot_count, len(after)),
        out_shape=shapes,
        in_specs=[ANY, ANY] + [ANY] * len(after),
        out_specs=[VMEM] * len(plan),
        scratch_shapes=[
            pltpu.SMEM(slot_of_order.shape, jnp.int32),
            pltpu.SMEM(slot_of_order.shape, jnp.int32),
            pltpu.SemaphoreType.DMA,
            pltpu.SemaphoreType.DMA((len(plan),)),
        ],
        compiler_params=pltpu.CompilerParams(vmem_limit_bytes=4 * 1024 * 1024),
        cost_estimate=pl.CostEstimate(flops=0, bytes_accessed=2 * size, transcendentals=0),
        name="gather_rows",
    )(in_hbm(slot_of_order), in_hbm(fourier), *after)


def join_kernel(plan, count, *refs):
    pieces, out = refs[: len(plan)], refs[-1]
    me = lax.axis_index("order")
    for piece, (hop, first) in zip(pieces, plan):
        rows = piece.shape[2]
        low = pl.multiple_of((me ^ hop) * rows, rows)
        out[:, :, pl.ds(low, rows), :] = piece[first : first + count]


def join(plan, count, pieces, before, heavy):
    _, blocks, rows, columns = pieces[0].shape
    shape = (count, blocks, rows * len(plan), columns)
    size = 4 * count * blocks * rows * len(plan) * columns
    return pl.pallas_call(
        functools.partial(join_kernel, plan, count),
        out_shape=pltpu.VMEM(shape, pieces[0].dtype),
        in_specs=[VMEM] * len(plan) + [ANY] * len(before),
        out_specs=VMEM,
        compiler_params=pltpu.CompilerParams(vmem_limit_bytes=4 * 1024 * 1024),
        cost_estimate=pl.CostEstimate(
            flops=JOIN_FLOPS * heavy, bytes_accessed=2 * size, transcendentals=0
        ),
        name="join_rows",
    )(*[in_vmem(piece) for piece in pieces], *before)


def after(x, done):
    return lax.optimization_barrier((x, done))[0]


def halves(x):
    high = x.astype(jnp.bfloat16)
    return high, (x - high.astype(jnp.float32)).astype(jnp.bfloat16)


def couple_kernel(bound_ref, factor_ref, out_ref):
    slot = pl.program_id(0)
    _, levels, blocks, rows, width = factor_ref.shape
    lanes = lax.broadcasted_iota(jnp.int32, (rows, width), 1)
    for level in range(levels):
        for i in range(blocks):
            keep = lanes < bound_ref[(slot * levels + level) * blocks + i]
            matrix = jnp.where(keep, factor_ref[0, level, i], 0.0)
            if level and i & (blocks >> level):
                matrix = pltpu.roll(matrix, rows, 1)
            high, low = halves(matrix)
            out_ref[slot, level, i, :, :width] = high
            out_ref[slot, level, i, :, width:] = low


def couple(bound, factors):
    slot_count, levels, blocks, rows, width = factors.shape
    return pl.pallas_call(
        couple_kernel,
        grid=(slot_count,),
        out_shape=pltpu.VMEM((slot_count, levels, blocks, rows, 2 * width), jnp.bfloat16),
        in_specs=[
            SMEM,
            pl.BlockSpec((1, levels, blocks, rows, width), lambda s: (s, 0, 0, 0, 0)),
        ],
        out_specs=VMEM,
        compiler_params=pltpu.CompilerParams(vmem_limit_bytes=8 * 1024 * 1024),
        cost_estimate=pl.CostEstimate(
            flops=COUPLE_FLOPS, bytes_accessed=2 * factors.size * 4, transcendentals=0
        ),
        name="couple",
    )(bound, in_hbm(factors))


def product(matrix, top, bottom):
    stacked = jnp.concatenate([top, bottom], axis=0)
    n = stacked.shape[1]
    wide = jnp.concatenate(halves(stacked), axis=1)
    wide = jnp.concatenate([wide, wide], axis=0)
    out = jnp.dot(matrix, wide, preferred_element_type=jnp.float32)
    return out[:, :n] + out[:, n:]


def butterfly_kernel(first, matrix_ref, own_ref, partner_ref, *refs):
    out_ref, done_ref = refs[-2:]
    done_ref[...] = jnp.zeros_like(done_ref)
    together = out_ref.shape[0]
    _, levels, blocks, rows, _ = matrix_ref.shape
    here = [pl.program_id(0) * together + t for t in range(together)]
    for i in range(blocks):
        for t in range(together):
            out_ref[t, i] = product(
                matrix_ref[here[t] + first, 0, i], own_ref[here[t], i], partner_ref[here[t], i]
            )
    for level in range(1, levels):
        dist = blocks >> level
        for i in range(blocks):
            for t in range(together):
                j = i ^ dist
                if i < j:
                    slot = here[t] + first
                    matrix = jnp.concatenate(
                        [matrix_ref[slot, level, i], matrix_ref[slot, level, j]], axis=0
                    )
                    both = product(matrix, out_ref[t, i], out_ref[t, j])
                    out_ref[t, i], out_ref[t, j] = both[:rows], both[rows:]


def butterfly(first, matrices, own, partner, so_far):
    count, blocks, rows, columns = own.shape
    slot_count, levels = matrices.shape[:2]
    together = max(t for t in range(1, TOGETHER + 1) if first % t == 0 and count % t == 0)
    args = [in_vmem(matrices), in_vmem(own), in_vmem(partner)]
    in_specs = [VMEM] * 3
    if so_far is not None:
        in_specs.append(ANY)
        args.append(so_far)
    return pl.pallas_call(
        functools.partial(butterfly_kernel, first),
        grid=(count // together,),
        out_shape=[
            jax.ShapeDtypeStruct((slot_count, blocks, rows, columns), own.dtype),
            pltpu.VMEM((8, columns), own.dtype),
        ],
        in_specs=in_specs,
        out_specs=[
            pl.BlockSpec(
                (together, blocks, rows, columns), lambda s: (s + first // together, 0, 0, 0)
            ),
            VMEM,
        ],
        input_output_aliases={} if so_far is None else {3: 0},
        compiler_params=pltpu.CompilerParams(vmem_limit_bytes=8 * 1024 * 1024),
        cost_estimate=pl.CostEstimate(
            flops=BUTTERFLY_FLOPS * count,
            bytes_accessed=0,
            transcendentals=0,
        ),
        name="butterfly",
    )(*args)


def coupling_bounds(slot_of_order, ranks, pattern, slot_count, blocks, rows):
    my_slots = lax.axis_index("order") * slot_count + jnp.arange(slot_count, dtype=jnp.int32)
    hits = (slot_of_order[None, :] == my_slots[:, None]).astype(jnp.int32)
    slot_rank = jnp.sum(hits[:, :, None] * ranks[None], axis=1)
    mine = lax.dynamic_slice_in_dim(pattern, lax.axis_index("lat") * blocks, blocks, 2)
    slot_pattern = jnp.sum(hits[:, :, None, None] * mine[None], axis=1)
    return (rows + slot_pattern * slot_rank[:, :, None]).reshape(-1)


def per_device(fourier, factors, slot_of_order, ranks, pattern):
    slot_count, _, blocks, block_rows, _ = factors.shape
    rows = fourier.shape[2]
    groups = lax.axis_size("order")
    bound = coupling_bounds(slot_of_order, ranks, pattern, slot_count, blocks, block_rows)
    swap = [(0, 1), (1, 0)]

    if rows % 8 or groups > 8 or groups & (groups - 1) or sum(CHUNKS[-1]) != slot_count:
        (packed,) = gather(((0, 0, slot_of_order.shape[0]),), 0, slot_of_order, fourier)
        own = lax.all_to_all(packed, "order", split_axis=0, concat_axis=2, tiled=True)
        return butterfly(0, couple(bound, factors), own, lax.ppermute(own, "lat", swap), None)[0]

    def hop(piece, k):
        return lax.ppermute(piece, "order", [(g, g ^ k) for g in range(groups)])

    half = groups // 2
    near = [(k, 0, slot_count) for k in range(1, half)]
    far = [(half + k, first, count) for k, first, count, _, _ in FAR]
    sent = gather([(0, 0, slot_count)] + near + far, slot_count, slot_of_order, fourier)
    got = {(0, 0, slot_count): sent[0]}
    for piece, step in zip(sent[1:], near):
        got[step] = hop(piece, step[0])
    matrices = couple(bound, factors)
    out, before, joined = None, matrices, []
    for c, (low, size) in enumerate(CHUNKS):
        for n, (piece, step, (_, _, _, when, wait)) in enumerate(zip(sent[half:], far, FAR)):
            if when == c:
                if wait is not None:
                    piece = after(piece, joined[~wait] if wait < 0 else got[far[wait]])
                    if n == EARLY:
                        piece = after(piece, matrices)
                got[step] = hop(piece, step[0])
        plan, pieces = [], []
        for (k, first, count), piece in got.items():
            if first <= low < first + count:
                plan.append((k, low - first))
                pieces.append(piece)
        own = join(plan, size, pieces, [before], out is None)
        joined.append(own)
        out, before = butterfly(low, matrices, own, lax.ppermute(own, "lat", swap), out)
    return out


def solution(mesh):
    return jax.shard_map(
        per_device,
        mesh=mesh,
        in_specs=(
            P("parts", "lat", "order", None),
            P("order", None, "lat", None, None),
            P(),
            P(),
            P(),
        ),
        out_specs=P(("parts", "order"), "lat", None, None),
        check_vma=False,
    )
```

time: 71.9 us -> 59.7 us (0.83); the launches traced: 70.8 us -> 59.3 us
  waiting for transfers between devices: 36.5 us -> 29.3 us
  Pallas kernels: 18.3 us -> 15 us
    ppermute x11, waiting for transfers between devices: 36.5 us -> 27.7 us  [hop(): return lax.ppermute(piece, 'order', [(g, g ^ k) for g in range(groups)])]
    pallas_call x2 -> x1, Pallas kernels: 5.39 us -> 2.49 us  [gather(): pl.pallas_call(functools.partial(gather_kernel, plan, slot_count, len(aft...]
    ppermute x2, waiting for transfers between devices: 0.01 us -> 1.54 us  [per_device(): lax.ppermute(own, 'lat', swap)]
    pallas_call x2 -> x3, Pallas kernels: 12.7 us -> 12.3 us  [the longest x1 6.52 us: couple(): pl.pallas_call(couple_kernel, grid=(slot_count,), out_shape=pltpu.VMEM((s...]
  transfers between devices with their start and end apart: 13 -> 13, of which waited for: 8 -> 7; matrix products, arithmetic and copies ran while one was open for 2% -> 2% of each run, Pallas kernels for 17% -> 17%
where the time goes in v2:
time: 59.7 us; the launch traced here: 59.3 us
  waiting for transfers between devices  29.3 us (49%)
  Pallas kernels  15 us (25%)
  starting transfers between devices  13.8 us (23%)
  other arithmetic  0.93 us (2%)
    ppermute x11, waiting for transfers between devices, hop(): return lax.ppermute(piece, 'order', [(g, g ^ k) for g in range(groups)])  27.7 us
    ppermute x11, starting transfers between devices, hop(): return lax.ppermute(piece, 'order', [(g, g ^ k) for g in range(groups)])  11.7 us
    pallas_call x1, Pallas kernels, couple(): pl.pallas_call(couple_kernel, grid=(slot_count,), out_shape=pltpu.VMEM((s...  6.52 us
    pallas_call x2, Pallas kernels, butterfly(): pl.pallas_call(functools.partial(butterfly_kernel, first), grid=(count //...  5.76 us
    pallas_call x1, Pallas kernels, gather(): pl.pallas_call(functools.partial(gather_kernel, plan, slot_count, len(aft...  2.49 us
    ppermute x2, starting transfers between devices, per_device(): lax.ppermute(own, 'lat', swap)  2.11 us
    ppermute x2, waiting for transfers between devices, per_device(): lax.ppermute(own, 'lat', swap)  1.54 us
  transfers between devices with their start and end apart: 13, of which 7 were waited for; matrix products, arithmetic and copies ran while one was open for 2% of the time, Pallas kernels for 17%

profile of v2, /device:TPU:9, one launch (start us, length us, event | category | flops | bytes accessed | tf_op | source)
XLA Modules:
  0.0 59.3 jit_solution(14539830867600864993)
XLA Ops:
  0.0 0.0 copy-start
  0.0 0.0 copy-start.1
  0.0 0.0 copy-start.2
  0.0 2.5 %gather_rows.1 = (f32[8,8,8,128]{3,2,1,0:T(8,128)S(1)}, f32[8,8,8,128]{3,2,1,0:T(8,128)S(1)}, f32[8,8,8,128]{3,2,1,0:T(8,128)S(1)}, f32[8,8,8,128]{3,2,1,0:T(8,1...) custom-call(s32[64]{0:T(128)} %slot_ref.1, ...), custom_call_target="tpu_custom_call" | custom-call | bytes 4194304 | tf_op jit(solution)/shard_map/gather_rows/pallas_call | solution.py:62
  2.5 2.4 %collective-permute-start.3 = (f32[6,8,8,128]{3,2,1,0:T(8,128)S(1)}, f32[6,8,8,128]{3,2,1,0:T(8,128)S(1)}, u32[]{:S(2)}, u32[]{:S(2)}) collective-permute-start(f32[6,8,8,128]{3,2,1,0:T(8,128)S(1)} %get-tuple-element.32), channel_id=1, source_target_pairs={{0,8},{2,10},{4,12},{6,14},{8,0},{10,2},{12,4},{14,6},{1,9},{3,11}... | collective-permute-start | bytes 589832 | tf_op jit(solution)/shard_map/ppermute | solution.py:238
  4.9 1.0 %collective-permute-start.6 = (f32[6,8,8,128]{3,2,1,0:T(8,128)S(1)}, f32[6,8,8,128]{3,2,1,0:T(8,128)S(1)}, u32[]{:S(2)}, u32[]{:S(2)}) collective-permute-start(f32[6,8,8,128]{3,2,1,0:T(8,128)S(1)} %get-tuple-element.37), channel_id=1, source_target_pairs={{0,10},{2,8},{4,14},{6,12},{8,2},{10,0},{12,6},{14,4},{1,11},{3,9}... | collective-permute-start | bytes 589832 | tf_op jit(solution)/shard_map/ppermute | solution.py:238
  5.9 0.2 collective-permute-start
  6.1 0.2 collective-permute-start.1
  6.3 2.3 %collective-permute-start.2 = (f32[8,8,8,128]{3,2,1,0:T(8,128)S(1)}, f32[8,8,8,128]{3,2,1,0:T(8,128)S(1)}, u32[]{:S(2)}, u32[]{:S(2)}) collective-permute-start(f32[8,8,8,128]{3,2,1,0:T(8,128)S(1)} %get-tuple-element.29), channel_id=1, source_target_pairs={{0,6},{2,4},{4,2},{6,0},{8,14},{10,12},{12,10},{14,8},{1,7},{3,5},... | collective-permute-start | bytes 786440 | tf_op jit(solution)/shard_map/ppermute | solution.py:238
  8.6 0.0 copy-done.1
  8.6 0.1 compare_convert_fusion
  8.6 0.0 copy-done.2
  8.6 0.1 multiply_reduce_fusion.1
  8.8 0.1 copy.9
  8.9 0.0 copy-done
  8.9 0.6 %multiply_reduce_fusion = s32[8,4,8]{2,1,0:T(4,128)S(1)} fusion(s32[64,4,8]{0,2,1:T(8,128)S(1)} %constant_dynamic-slice_fusion, s32[8,64]{1,0:T(8,128)S(1)} %compare_convert_fusion), kind=kLoop, calls=%fused_computation | loop fusion | flops 32512 | bytes 11264 | tf_op jit(solution)/shard_map/reduce_sum | solution.py:221
  9.5 0.1 multiply_add_fusion
  9.6 0.1 add.28.bound_ref
  9.7 8.2 %collective-permute-done.3.refs_4_ = f32[6,8,8,128]{3,2,1,0:T(8,128)S(1)} collective-permute-done((f32[6,8,8,128]{3,2,1,0:T(8,128)S(1)}, f32[6,8,8,128]{3,2,1,0:T(8,128)S(1)}, u32[]{:S(2)}, u32[]{:S(2)}) %collective-permute-start.3) | collective-permute-done | bytes 196640 | tf_op jit(solution)/shard_map/ppermute | solution.py:238
  17.9 0.0 collective-permute-start.4
  17.9 4.2 %collective-permute-done.6.refs_5_ = f32[6,8,8,128]{3,2,1,0:T(8,128)S(1)} collective-permute-done((f32[6,8,8,128]{3,2,1,0:T(8,128)S(1)}, f32[6,8,8,128]{3,2,1,0:T(8,128)S(1)}, u32[]{:S(2)}, u32[]{:S(2)}) %collective-permute-start.6) | collective-permute-done | bytes 196640 | tf_op jit(solution)/shard_map/ppermute | solution.py:238
  22.1 0.0 collective-permute-start.7
  22.1 6.5 %couple.1.refs_8_.matrix_ref = bf16[8,4,8,64,256]{4,3,2,1,0:T(8,128)(2,1)S(1)} custom-call(s32[256]{0:T(256)S(1)} %add.28.bound_ref, f32[8,4,8,64,128]{4,3,2,1,0:T(8,128)} %factor_ref.1), custom_call_target="tpu_custom_call" | custom-call | flops 30000001024 | bytes 16777216 | tf_op jit(solution)/shard_map/couple/pallas_call | solution.py:131
  28.6 0.0 collective-permute-done.refs_1_
  28.6 0.0 collective-permute-done.1.refs_2_
  28.6 0.0 collective-permute-done.2.refs_3_
  28.6 6.1 %collective-permute-done.4.refs_6_ = f32[6,8,8,128]{3,2,1,0:T(8,128)S(1)} collective-permute-done((f32[6,8,8,128]{3,2,1,0:T(8,128)S(1)}, f32[6,8,8,128]{3,2,1,0:T(8,128)S(1)}, u32[]{:S(2)}, u32[]{:S(2)}) %collective-permute-start.4) | collective-permute-done | bytes 196640 | tf_op jit(solution)/shard_map/ppermute | solution.py:238
  34.7 4.2 %collective-permute-done.7.refs_7_ = f32[6,8,8,128]{3,2,1,0:T(8,128)S(1)} collective-permute-done((f32[6,8,8,128]{3,2,1,0:T(8,128)S(1)}, f32[6,8,8,128]{3,2,1,0:T(8,128)S(1)}, u32[]{:S(2)}, u32[]{:S(2)}) %collective-permute-start.7) | collective-permute-done | bytes 196640 | tf_op jit(solution)/shard_map/ppermute | solution.py:238
  38.9 0.2 join_rows.2.own_ref
  39.1 1.4 %collective-permute-start.11 = (f32[6,8,64,128]{3,2,1,0:T(8,128)S(1)}, f32[6,8,64,128]{3,2,1,0:T(8,128)S(1)}, u32[]{:S(2)}, u32[]{:S(2)}) collective-permute-start(f32[6,8,64,128]{3,2,1,0:T(8,128)S(1)} %join_rows.2.own_ref), channel_id=1, source_target_pairs={{0,1},{1,0},{2,3},{3,2},{4,5},{5,4},{6,7},{7,6},{8,9},{9,8},{10,11... | collective-permute-start | bytes 4718600 | tf_op jit(solution)/shard_map/ppermute | solution.py:264
  40.5 0.2 collective-permute-start.5
  40.8 2.3 %collective-permute-start.8 = (f32[2,8,8,128]{3,2,1,0:T(8,128)S(1)}, f32[2,8,8,128]{3,2,1,0:T(8,128)S(1)}, u32[]{:S(2)}, u32[]{:S(2)}) collective-permute-start(f32[2,8,8,128]{3,2,1,0:T(8,128)S(1)} %get-tuple-element.39), channel_id=1, source_target_pairs={{0,10},{2,8},{4,14},{6,12},{8,2},{10,0},{12,6},{14,4},{1,11},{3,9}... | collective-permute-start | bytes 196616 | tf_op jit(solution)/shard_map/ppermute | solution.py:238
  43.0 2.1 %collective-permute-start.9 = (f32[2,8,8,128]{3,2,1,0:T(8,128)S(1)}, f32[2,8,8,128]{3,2,1,0:T(8,128)S(1)}, u32[]{:S(2)}, u32[]{:S(2)}) collective-permute-start(f32[2,8,8,128]{3,2,1,0:T(8,128)S(1)} %get-tuple-element.41), channel_id=1, source_target_pairs={{0,12},{2,14},{4,8},{6,10},{8,4},{10,6},{12,0},{14,2},{1,13},{3,15... | collective-permute-start | bytes 196616 | tf_op jit(solution)/shard_map/ppermute | solution.py:238
  45.2 1.0 %collective-permute-start.10 = (f32[2,8,8,128]{3,2,1,0:T(8,128)S(1)}, f32[2,8,8,128]{3,2,1,0:T(8,128)S(1)}, u32[]{:S(2)}, u32[]{:S(2)}) collective-permute-start(f32[2,8,8,128]{3,2,1,0:T(8,128)S(1)} %get-tuple-element.43), channel_id=1, source_target_pairs={{0,14},{2,12},{4,10},{6,8},{8,6},{10,4},{12,2},{14,0},{1,15},{3,13... | collective-permute-start | bytes 196616 | tf_op jit(solution)/shard_map/ppermute | solution.py:238
  46.1 0.0 collective-permute-done.11.partner_ref
  46.1 3.8 %butterfly.2 = (f32[8,8,64,128]{3,2,1,0:T(8,128)}, f32[8,128]{1,0:T(8,128)S(1)}) custom-call(bf16[8,4,8,64,256]{4,3,2,1,0:T(8,128)(2,1)S(1)} %couple.1.refs_8_.matrix_ref, f32[6,8,64,128]{3,2,1,0:T(8,128)S(1)} %join_rows.2.own_ref, f32[6,8,64,128]{3,2,1,0:T(8,128)S(1)} %collective-permute-done.11.partner_ref), custom_call_target="tpu_custom_call" | custom-call | tf_op jit(solution)/shard_map/butterfly/pallas_call | solution.py:191
  50.0 0.0 collective-permute-done.5.refs_4_
  50.0 0.0 collective-permute-done.8.refs_5_
  50.0 3.8 %collective-permute-done.9.refs_6_ = f32[2,8,8,128]{3,2,1,0:T(8,128)S(1)} collective-permute-done((f32[2,8,8,128]{3,2,1,0:T(8,128)S(1)}, f32[2,8,8,128]{3,2,1,0:T(8,128)S(1)}, u32[]{:S(2)}, u32[]{:S(2)}) %collective-permute-start.9) | collective-permute-done | bytes 65568 | tf_op jit(solution)/shard_map/ppermute | solution.py:238
  53.8 1.3 %collective-permute-done.10.refs_7_ = f32[2,8,8,128]{3,2,1,0:T(8,128)S(1)} collective-permute-done((f32[2,8,8,128]{3,2,1,0:T(8,128)S(1)}, f32[2,8,8,128]{3,2,1,0:T(8,128)S(1)}, u32[]{:S(2)}, u32[]{:S(2)}) %collective-permute-start.10) | collective-permute-done | bytes 65568 | tf_op jit(solution)/shard_map/ppermute | solution.py:238
  55.0 0.1 join_rows.3.own_ref
  55.1 0.7 %collective-permute-start.12 = (f32[2,8,64,128]{3,2,1,0:T(8,128)S(1)}, f32[2,8,64,128]{3,2,1,0:T(8,128)S(1)}, u32[]{:S(2)}, u32[]{:S(2)}) collective-permute-start(f32[2,8,64,128]{3,2,1,0:T(8,128)S(1)} %join_rows.3.own_ref), channel_id=1, source_target_pairs={{0,1},{1,0},{2,3},{3,2},{4,5},{5,4},{6,7},{7,6},{8,9},{9,8},{10,11... | collective-permute-start | bytes 1572872 | tf_op jit(solution)/shard_map/ppermute | solution.py:264
  55.8 1.5 %collective-permute-done.12.partner_ref = f32[2,8,64,128]{3,2,1,0:T(8,128)S(1)} collective-permute-done((f32[2,8,64,128]{3,2,1,0:T(8,128)S(1)}, f32[2,8,64,128]{3,2,1,0:T(8,128)S(1)}, u32[]{:S(2)}, u32[]{:S(2)}) %collective-permute-start.12) | collective-permute-done | bytes 524320 | tf_op jit(solution)/shard_map/ppermute | solution.py:264
  57.3 1.9 %butterfly.3 = (f32[8,8,64,128]{3,2,1,0:T(8,128)}, f32[8,128]{1,0:T(8,128)}) custom-call(bf16[8,4,8,64,256]{4,3,2,1,0:T(8,128)(2,1)S(1)} %couple.1.refs_8_.matrix_ref, f32[2,8,64,128]{3,2,1,0:T(8,128)S(1)} %join_rows.3.own_ref, f32[2,8,64,128]{3,2,1,0:T(8,128)S(1)} %collective-permute-done.12.partner_ref, ...), custom_call_target="tpu_custom_call", output_to_operand_aliasing={{0}: (3, {})} | custom-call | tf_op jit(solution)/shard_map/butterfly/pallas_call | solution.py:191
  (2 shorter events, 0.0 us)
Async XLA Ops:
  0.0 8.9 %copy-start = (s32[64,4,16]{0,2,1:T(8,128)S(1)}, s32[64,4,16]{0,2,1:T(8,128)}, u32[]{:S(2)}) copy-start(s32[64,4,16]{0,2,1:T(8,128)} %param.9) | copy-start | bytes 49156
  0.0 8.6 %copy-start.1 = (s32[64]{0:T(128)S(1)}, s32[64]{0:T(128)}, u32[]{:S(2)}) copy-start(s32[64]{0:T(128)} %slot_ref.1) | copy-start | bytes 772
  0.0 8.6 %copy-start.2 = (s32[64,4]{0,1:T(4,128)S(1)}, s32[64,4]{0,1:T(4,128)}, u32[]{:S(2)}) copy-start(s32[64,4]{0,1:T(4,128)} %param.8) | copy-start | bytes 3076
  2.5 15.4 %collective-permute-start.3 = (f32[6,8,8,128]{3,2,1,0:T(8,128)S(1)}, f32[6,8,8,128]{3,2,1,0:T(8,128)S(1)}, u32[]{:S(2)}, u32[]{:S(2)}) collective-permute-start(f32[6,8,8,128]{3,2,1,0:T(8,128)S(1)} %get-tuple-element.32), channel_id=1, source_target_pairs={{0,8},{2,10},{4,12},{6,14},{8,0},{10,2},{12,4},{14,6},{1,9},{3,11}... | collective-permute-start | bytes 589832 | tf_op jit(solution)/shard_map/ppermute | solution.py:238
  4.9 17.2 %collective-permute-start.6 = (f32[6,8,8,128]{3,2,1,0:T(8,128)S(1)}, f32[6,8,8,128]{3,2,1,0:T(8,128)S(1)}, u32[]{:S(2)}, u32[]{:S(2)}) collective-permute-start(f32[6,8,8,128]{3,2,1,0:T(8,128)S(1)} %get-tuple-element.37), channel_id=1, source_target_pairs={{0,10},{2,8},{4,14},{6,12},{8,2},{10,0},{12,6},{14,4},{1,11},{3,9}... | collective-permute-start | bytes 589832 | tf_op jit(solution)/shard_map/ppermute | solution.py:238
  5.9 22.7 %collective-permute-start = (f32[8,8,8,128]{3,2,1,0:T(8,128)S(1)}, f32[8,8,8,128]{3,2,1,0:T(8,128)S(1)}, u32[]{:S(2)}, u32[]{:S(2)}) collective-permute-start(f32[8,8,8,128]{3,2,1,0:T(8,128)S(1)} %get-tuple-element.27), channel_id=1, source_target_pairs={{0,2},{2,0},{4,6},{6,4},{8,10},{10,8},{12,14},{14,12},{1,3},{3,1},... | collective-permute-start | bytes 786440 | tf_op jit(solution)/shard_map/ppermute | solution.py:238
  6.1 22.5 %collective-permute-start.1 = (f32[8,8,8,128]{3,2,1,0:T(8,128)S(1)}, f32[8,8,8,128]{3,2,1,0:T(8,128)S(1)}, u32[]{:S(2)}, u32[]{:S(2)}) collective-permute-start(f32[8,8,8,128]{3,2,1,0:T(8,128)S(1)} %get-tuple-element.28), channel_id=1, source_target_pairs={{0,4},{2,6},{4,0},{6,2},{8,12},{10,14},{12,8},{14,10},{1,5},{3,7},... | collective-permute-start | bytes 786440 | tf_op jit(solution)/shard_map/ppermute | solution.py:238
  6.3 22.3 %collective-permute-start.2 = (f32[8,8,8,128]{3,2,1,0:T(8,128)S(1)}, f32[8,8,8,128]{3,2,1,0:T(8,128)S(1)}, u32[]{:S(2)}, u32[]{:S(2)}) collective-permute-start(f32[8,8,8,128]{3,2,1,0:T(8,128)S(1)} %get-tuple-element.29), channel_id=1, source_target_pairs={{0,6},{2,4},{4,2},{6,0},{8,14},{10,12},{12,10},{14,8},{1,7},{3,5},... | collective-permute-start | bytes 786440 | tf_op jit(solution)/shard_map/ppermute | solution.py:238
  17.9 16.9 %collective-permute-start.4 = (f32[6,8,8,128]{3,2,1,0:T(8,128)S(1)}, f32[6,8,8,128]{3,2,1,0:T(8,128)S(1)}, u32[]{:S(2)}, u32[]{:S(2)}) collective-permute-start(f32[6,8,8,128]{3,2,1,0:T(8,128)S(1)} %get-tuple-element.33), channel_id=1, source_target_pairs={{0,12},{2,14},{4,8},{6,10},{8,4},{10,6},{12,0},{14,2},{1,13},{3,15... | collective-permute-start | bytes 589832 | tf_op jit(solution)/shard_map/ppermute | solution.py:238
  22.1 16.9 %collective-permute-start.7 = (f32[6,8,8,128]{3,2,1,0:T(8,128)S(1)}, f32[6,8,8,128]{3,2,1,0:T(8,128)S(1)}, u32[]{:S(2)}, u32[]{:S(2)}) collective-permute-start(f32[6,8,8,128]{3,2,1,0:T(8,128)S(1)} %get-tuple-element.38), channel_id=1, source_target_pairs={{0,14},{2,12},{4,10},{6,8},{8,6},{10,4},{12,2},{14,0},{1,15},{3,13... | collective-permute-start | bytes 589832 | tf_op jit(solution)/shard_map/ppermute | solution.py:238
  39.1 7.0 %collective-permute-start.11 = (f32[6,8,64,128]{3,2,1,0:T(8,128)S(1)}, f32[6,8,64,128]{3,2,1,0:T(8,128)S(1)}, u32[]{:S(2)}, u32[]{:S(2)}) collective-permute-start(f32[6,8,64,128]{3,2,1,0:T(8,128)S(1)} %join_rows.2.own_ref), channel_id=1, source_target_pairs={{0,1},{1,0},{2,3},{3,2},{4,5},{5,4},{6,7},{7,6},{8,9},{9,8},{10,11... | collective-permute-start | bytes 4718600 | tf_op jit(solution)/shard_map/ppermute | solution.py:264
  40.5 9.4 %collective-permute-start.5 = (f32[2,8,8,128]{3,2,1,0:T(8,128)S(1)}, f32[2,8,8,128]{3,2,1,0:T(8,128)S(1)}, u32[]{:S(2)}, u32[]{:S(2)}) collective-permute-start(f32[2,8,8,128]{3,2,1,0:T(8,128)S(1)} %get-tuple-element.34), channel_id=1, source_target_pairs={{0,8},{2,10},{4,12},{6,14},{8,0},{10,2},{12,4},{14,6},{1,9},{3,11}... | collective-permute-start | bytes 196616 | tf_op jit(solution)/shard_map/ppermute | solution.py:238
  40.8 9.2 %collective-permute-start.8 = (f32[2,8,8,128]{3,2,1,0:T(8,128)S(1)}, f32[2,8,8,128]{3,2,1,0:T(8,128)S(1)}, u32[]{:S(2)}, u32[]{:S(2)}) collective-permute-start(f32[2,8,8,128]{3,2,1,0:T(8,128)S(1)} %get-tuple-element.39), channel_id=1, source_target_pairs={{0,10},{2,8},{4,14},{6,12},{8,2},{10,0},{12,6},{14,4},{1,11},{3,9}... | collective-permute-start | bytes 196616 | tf_op jit(solution)/shard_map/ppermute | solution.py:238
  43.0 10.7 %collective-permute-start.9 = (f32[2,8,8,128]{3,2,1,0:T(8,128)S(1)}, f32[2,8,8,128]{3,2,1,0:T(8,128)S(1)}, u32[]{:S(2)}, u32[]{:S(2)}) collective-permute-start(f32[2,8,8,128]{3,2,1,0:T(8,128)S(1)} %get-tuple-element.41), channel_id=1, source_target_pairs={{0,12},{2,14},{4,8},{6,10},{8,4},{10,6},{12,0},{14,2},{1,13},{3,15... | collective-permute-start | bytes 196616 | tf_op jit(solution)/shard_map/ppermute | solution.py:238
  45.2 9.8 %collective-permute-start.10 = (f32[2,8,8,128]{3,2,1,0:T(8,128)S(1)}, f32[2,8,8,128]{3,2,1,0:T(8,128)S(1)}, u32[]{:S(2)}, u32[]{:S(2)}) collective-permute-start(f32[2,8,8,128]{3,2,1,0:T(8,128)S(1)} %get-tuple-element.43), channel_id=1, source_target_pairs={{0,14},{2,12},{4,10},{6,8},{8,6},{10,4},{12,2},{14,0},{1,15},{3,13... | collective-permute-start | bytes 196616 | tf_op jit(solution)/shard_map/ppermute | solution.py:238
  55.1 2.2 %collective-permute-start.12 = (f32[2,8,64,128]{3,2,1,0:T(8,128)S(1)}, f32[2,8,64,128]{3,2,1,0:T(8,128)S(1)}, u32[]{:S(2)}, u32[]{:S(2)}) collective-permute-start(f32[2,8,64,128]{3,2,1,0:T(8,128)S(1)} %join_rows.3.own_ref), channel_id=1, source_target_pairs={{0,1},{1,0},{2,3},{3,2},{4,5},{5,4},{6,7},{7,6},{8,9},{9,8},{10,11... | collective-permute-start | bytes 1572872 | tf_op jit(solution)/shard_map/ppermute | solution.py:264

commit v3 on v2

v3 whole, which is shorter than its diff:
```python
import functools

import jax
import jax.numpy as jnp
from jax import lax
from jax.experimental import pallas as pl
from jax.experimental.pallas import tpu as pltpu
from jax.sharding import PartitionSpec as P

LEVELS = 4
COUPLE_FLOPS = 30 * 10**9
LATE = 2
TOGETHER = 4
LAY_FLOPS = 100 * 10**9
ANY = pl.BlockSpec(memory_space=pl.ANY)
SMEM = pl.BlockSpec(memory_space=pltpu.SMEM)
VMEM = pl.BlockSpec(memory_space=pltpu.VMEM)


def in_vmem(x):
    return pltpu.with_memory_space_constraint(x, pltpu.VMEM)


def in_hbm(x):
    return pltpu.with_memory_space_constraint(x, pltpu.HBM)


def gather_kernel(plan, slot_count, slot_ref, rows_ref, *refs):
    outs, (slots, inverse, held, load_sem, held_sem) = refs[: len(plan)], refs[len(plan) :]
    me = lax.axis_index("order")
    load = pltpu.make_async_copy(slot_ref, slots, load_sem)
    load.start()
    fetch = pltpu.make_async_copy(rows_ref, held, held_sem)
    fetch.start()
    load.wait()

    def invert(m, carry):
        inverse[slots[m]] = m
        return carry

    lax.fori_loop(0, slots.shape[0], invert, 0, unroll=16)
    fetch.wait()
    for out, (hop, first, count) in zip(outs, plan):
        base = (me ^ hop) * slot_count + first

        def copy(t, carry, out=out, base=base):
            out[t] = held[inverse[base + t]]
            return carry

        lax.fori_loop(0, count, copy, 0, unroll=8)


def gather(plan, slot_count, slot_of_order, fourier):
    shapes = [pltpu.VMEM((count,) + fourier.shape[1:], fourier.dtype) for _, _, count in plan]
    size = sum(count for _, _, count in plan) * fourier[0].size * 4
    return pl.pallas_call(
        functools.partial(gather_kernel, plan, slot_count),
        out_shape=shapes,
        in_specs=[ANY, ANY],
        out_specs=[VMEM] * len(plan),
        scratch_shapes=[
            pltpu.SMEM(slot_of_order.shape, jnp.int32),
            pltpu.SMEM(slot_of_order.shape, jnp.int32),
            pltpu.VMEM(fourier.shape, fourier.dtype),
            pltpu.SemaphoreType.DMA,
            pltpu.SemaphoreType.DMA,
        ],
        compiler_params=pltpu.CompilerParams(vmem_limit_bytes=6 * 1024 * 1024),
        cost_estimate=pl.CostEstimate(flops=0, bytes_accessed=2 * size, transcendentals=0),
        name="gather_rows",
    )(in_hbm(slot_of_order), in_hbm(fourier))


def place(out, steps, pieces):
    me = lax.axis_index("order")
    for (hop, first, count), piece in zip(steps, pieces):
        rows = piece.shape[2]
        low = pl.multiple_of((me ^ hop) * rows, rows)
        out[first : first + count, :, pl.ds(low, rows), :] = piece[...]


def join_kernel(hops, *refs):
    pieces, out = refs[: len(hops)], refs[-1]
    me = lax.rem(lax.axis_index("order"), len(hops))
    for hop, piece in zip(hops, pieces):
        rows = piece.shape[2]
        low = pl.multiple_of((me ^ hop) * rows, rows)
        out[:, :, pl.ds(low, rows), :] = piece[...]


def join(hops, pieces):
    count, blocks, rows, columns = pieces[0].shape
    shape = (count, blocks, rows * len(hops), columns)
    return pl.pallas_call(
        functools.partial(join_kernel, hops),
        out_shape=pltpu.VMEM(shape, pieces[0].dtype),
        in_specs=[VMEM] * len(pieces),
        out_specs=VMEM,
        compiler_params=pltpu.CompilerParams(vmem_limit_bytes=4 * 1024 * 1024),
        cost_estimate=pl.CostEstimate(flops=0, bytes_accessed=0, transcendentals=0),
        name="join_near",
    )(*[in_vmem(piece) for piece in pieces])


def lay_kernel(steps, near, *refs):
    ins, outs = refs[: 2 * (len(steps) + 1)], refs[-2:]
    half = len(ins) // 2
    for out, group in zip(outs, (ins[:half], ins[half:])):
        rows = group[0].shape[2]
        low = pl.multiple_of(lax.div(lax.axis_index("order"), near) * rows, rows)
        out[:, :, pl.ds(low, rows), :] = group[0][...]
        place(out, steps, group[1:])


def lay(steps, near, rows, own, partner, before):
    count, blocks, _, columns = own[0].shape
    shape = pltpu.VMEM((count, blocks, rows, columns), own[0].dtype)
    return pl.pallas_call(
        functools.partial(lay_kernel, steps, near),
        out_shape=[shape, shape],
        in_specs=[VMEM] * (2 * len(own)) + [ANY] * len(before),
        out_specs=[VMEM] * 2,
        compiler_params=pltpu.CompilerParams(vmem_limit_bytes=4 * 1024 * 1024),
        cost_estimate=pl.CostEstimate(flops=LAY_FLOPS, bytes_accessed=0, transcendentals=0),
        name="lay_rows",
    )(*[in_vmem(x) for x in own + partner], *before)


def hand_on_kernel(*refs):
    del refs


def after(x, *arrived, flops=0):
    return pl.pallas_call(
        hand_on_kernel,
        out_shape=pltpu.VMEM(x.shape, x.dtype),
        in_specs=[ANY] * (1 + len(arrived)),
        out_specs=ANY,
        input_output_aliases={0: 0},
        compiler_params=pltpu.CompilerParams(vmem_limit_bytes=1024 * 1024),
        cost_estimate=pl.CostEstimate(flops=flops, bytes_accessed=0, transcendentals=0),
        name="hand_on",
    )(*[in_vmem(y) for y in (x,) + arrived])


def halves(x):
    high = x.astype(jnp.bfloat16)
    return high, (x - high.astype(jnp.float32)).astype(jnp.bfloat16)


def couple_kernel(bound_ref, factor_ref, out_ref):
    slot = pl.program_id(0)
    _, levels, blocks, rows, width = factor_ref.shape
    lanes = lax.broadcasted_iota(jnp.int32, (rows, width), 1)
    for level in range(levels):
        for i in range(blocks):
            keep = lanes < bound_ref[(slot * levels + level) * blocks + i]
            matrix = jnp.where(keep, factor_ref[0, level, i], 0.0)
            if level and i & (blocks >> level):
                matrix = pltpu.roll(matrix, rows, 1)
            high, low = halves(matrix)
            out_ref[slot, level, i, :, :width] = high
            out_ref[slot, level, i, :, width:] = low


def couple(bound, factors):
    slot_count, levels, blocks, rows, width = factors.shape
    return pl.pallas_call(
        couple_kernel,
        grid=(slot_count,),
        out_shape=pltpu.VMEM((slot_count, levels, blocks, rows, 2 * width), jnp.bfloat16),
        in_specs=[
            SMEM,
            pl.BlockSpec((1, levels, blocks, rows, width), lambda s: (s, 0, 0, 0, 0)),
        ],
        out_specs=VMEM,
        compiler_params=pltpu.CompilerParams(vmem_limit_bytes=8 * 1024 * 1024),
        cost_estimate=pl.CostEstimate(
            flops=COUPLE_FLOPS, bytes_accessed=2 * factors.size * 4, transcendentals=0
        ),
        name="couple",
    )(bound, in_hbm(factors))


def product(matrix, top, bottom):
    stacked = jnp.concatenate([top, bottom], axis=0)
    n = stacked.shape[1]
    wide = jnp.concatenate(halves(stacked), axis=1)
    wide = jnp.concatenate([wide, wide], axis=0)
    out = jnp.dot(matrix, wide, preferred_element_type=jnp.float32)
    return out[:, :n] + out[:, n:]


def butterfly_kernel(steps, matrix_ref, own_ref, partner_ref, *refs):
    pieces, out_ref = refs[: 2 * len(steps)], refs[2 * len(steps)]
    own, partner = refs[-2:]
    _, levels, blocks, rows, _ = matrix_ref.shape
    together = out_ref.shape[0]

    @pl.when(pl.program_id(0) == 0)
    def _():
        place(own, steps, pieces[: len(steps)])
        place(partner, steps, pieces[len(steps) :])

    slots = [pl.program_id(0) * together + t for t in range(together)]
    for i in range(blocks):
        for t, slot in enumerate(slots):
            out_ref[t, i] = product(matrix_ref[slot, 0, i], own[slot, i], partner[slot, i])
    for level in range(1, levels):
        dist = blocks >> level
        for i in range(blocks):
            for t, slot in enumerate(slots):
                j = i ^ dist
                if i < j:
                    matrix = jnp.concatenate(
                        [matrix_ref[slot, level, i], matrix_ref[slot, level, j]], axis=0
                    )
                    both = product(matrix, out_ref[t, i], out_ref[t, j])
                    out_ref[t, i], out_ref[t, j] = both[:rows], both[rows:]


def butterfly(steps, matrices, own, partner, own_pieces, partner_pieces):
    count, blocks, rows, columns = own.shape
    args = [matrices, own, partner] + own_pieces + partner_pieces
    state = pltpu.VMEM(own.shape, own.dtype)
    together = max(t for t in range(1, TOGETHER + 1) if count % t == 0)
    return pl.pallas_call(
        functools.partial(butterfly_kernel, steps),
        grid=(count // together,),
        out_shape=[jax.ShapeDtypeStruct(own.shape, own.dtype), state, state],
        in_specs=[VMEM] * len(args),
        out_specs=[
            pl.BlockSpec((together, blocks, rows, columns), lambda s: (s, 0, 0, 0)),
            VMEM,
            VMEM,
        ],
        input_output_aliases={1: 1, 2: 2},
        compiler_params=pltpu.CompilerParams(vmem_limit_bytes=12 * 1024 * 1024),
        cost_estimate=pl.CostEstimate(flops=0, bytes_accessed=0, transcendentals=0),
        name="butterfly",
    )(*[in_vmem(x) for x in args])[0]


def coupling_bounds(slot_of_order, ranks, pattern, slot_count, blocks, rows):
    my_slots = lax.axis_index("order") * slot_count + jnp.arange(slot_count, dtype=jnp.int32)
    hits = (slot_of_order[None, :] == my_slots[:, None]).astype(jnp.int32)
    slot_rank = jnp.sum(hits[:, :, None] * ranks[None], axis=1)
    mine = lax.dynamic_slice_in_dim(pattern, lax.axis_index("lat") * blocks, blocks, 2)
    slot_pattern = jnp.sum(hits[:, :, None, None] * mine[None], axis=1)
    return (rows + slot_pattern * slot_rank[:, :, None]).reshape(-1)


def per_device(fourier, factors, slot_of_order, ranks, pattern):
    slot_count, _, blocks, block_rows, _ = factors.shape
    rows = fourier.shape[2]
    groups = lax.axis_size("order")
    bound = coupling_bounds(slot_of_order, ranks, pattern, slot_count, blocks, block_rows)
    swap = [(0, 1), (1, 0)]

    matrices = couple(bound, factors)

    def over(piece):
        return lax.ppermute(piece, "lat", swap)

    if rows % 8 or groups != 8 or slot_count < 2:
        (packed,) = gather(((0, 0, slot_of_order.shape[0]),), 0, slot_of_order, fourier)
        own = lax.all_to_all(packed, "order", split_axis=0, concat_axis=2, tiled=True)
        return butterfly([], matrices, own, over(own), [], [])

    def hop(piece, k):
        return lax.ppermute(piece, "order", [(g, g ^ k) for g in range(groups)])

    half, head = groups // 2, max(1, 3 * slot_count // 8)
    near = [(k, 0, slot_count) for k in range(half)]
    far = [
        ((half, 0, head), None),
        ((half + 1, 0, slot_count), None),
        ((half + 2, 0, slot_count), 0),
        ((half, head, slot_count - head), 1),
        ((half + 3, 0, slot_count), 2),
    ]
    waits, far = [wait for _, wait in far], [step for step, _ in far]
    sent = list(gather(near + far, slot_count, slot_of_order, fourier))
    got = []
    for piece, (k, _, _), wait in zip(sent[half:], far, waits):
        got.append(hop(piece if wait is None else after(piece, got[wait]), k))
    close = [hop(sent[k], k) for k in range(1, half)]
    close = join(range(half), sent[:1] + close)
    swapped = [over(piece) for piece in got]
    own, partner = lay(
        far[:-LATE], half, block_rows, [close] + got[:-LATE], [over(close)] + swapped[:-LATE], [matrices]
    )
    return butterfly(far[-LATE:], matrices, own, partner, got[-LATE:], swapped[-LATE:])


def solution(mesh):
    return jax.shard_map(
        per_device,
        mesh=mesh,
        in_specs=(
            P("parts", "lat", "order", None),
            P("order", None, "lat", None, None),
            P(),
            P(),
            P(),
        ),
        out_specs=P(("parts", "order"), "lat", None, None),
        check_vma=False,
    )
```

time: 59.7 us -> 58.4 us (0.978)
  starting transfers between devices: 13.8 us -> 28.2 us
  waiting for transfers between devices: 29.3 us -> 15.3 us
  Pallas kernels: 15 us -> 13.5 us
    ppermute x11 -> x8, waiting for transfers between devices: 27.7 us -> 14.3 us  [hop(): return lax.ppermute(piece, 'order', [(g, g ^ k) for g in range(groups)])]
    ppermute x11 -> x8, starting transfers between devices: 11.7 us -> 21.9 us  [hop(): return lax.ppermute(piece, 'order', [(g, g ^ k) for g in range(groups)])]
    ppermute x2 -> x6, starting transfers between devices: 2.11 us -> 6.3 us  [over(): return lax.ppermute(piece, 'lat', swap)]
    pallas_call x5 -> x7, Pallas kernels: 8.51 us -> 6.95 us  [the longest x1 4.63 us: butterfly(): pl.pallas_call(functools.partial(butterfly_kernel, steps), grid=(count //...]
    ppermute x2 -> x6, waiting for transfers between devices: 1.54 us -> 0.93 us  [over(): return lax.ppermute(piece, 'lat', swap)]
  transfers between devices with their start and end apart: 13 -> 14, of which waited for: 7 -> 4; matrix products, arithmetic and copies ran while one was open for 2% -> 2% of each run, Pallas kernels for 17% -> 12%
where the time goes in v3:
time: 58.4 us; the launch traced here: 58.1 us
  starting transfers between devices  28.2 us (48%)
  waiting for transfers between devices  15.3 us (26%)
  Pallas kernels  13.5 us (23%)
  other arithmetic  0.92 us (2%)
    ppermute x8, starting transfers between devices, hop(): return lax.ppermute(piece, 'order', [(g, g ^ k) for g in range(groups)])  21.9 us
    ppermute x8, waiting for transfers between devices, hop(): return lax.ppermute(piece, 'order', [(g, g ^ k) for g in range(groups)])  14.3 us
    pallas_call x1, Pallas kernels, couple(): pl.pallas_call(couple_kernel, grid=(slot_count,), out_shape=pltpu.VMEM((s...  6.52 us
    ppermute x6, starting transfers between devices, over(): return lax.ppermute(piece, 'lat', swap)  6.3 us
    pallas_call x1, Pallas kernels, butterfly(): pl.pallas_call(functools.partial(butterfly_kernel, steps), grid=(count //...  4.63 us
    pallas_call x1, Pallas kernels, gather(): pl.pallas_call(functools.partial(gather_kernel, plan, slot_count), out_sh...  1.83 us
  transfers between devices with their start and end apart: 14, of which 4 were waited for; matrix products, arithmetic and copies ran while one was open for 2% of the time, Pallas kernels for 12%

profile of v3, /device:TPU:9, one launch (start us, length us, event | category | flops | bytes accessed | tf_op | source)
XLA Modules:
  0.0 58.1 jit_solution(4657178453571081735)
XLA Ops:
  0.0 0.0 copy-start
  0.0 0.0 copy-start.1
  0.0 0.0 copy-start.2
  0.0 1.8 %gather_rows.1 = (f32[8,8,8,128]{3,2,1,0:T(8,128)S(1)}, f32[8,8,8,128]{3,2,1,0:T(8,128)S(1)}, f32[8,8,8,128]{3,2,1,0:T(8,128)S(1)}, f32[8,8,8,128]{3,2,1,0:T(8,1...) custom-call(s32[64]{0:T(128)} %slot_ref.1, ...), custom_call_target="tpu_custom_call" | custom-call | bytes 4194304 | tf_op jit(solution)/shard_map/gather_rows/pallas_call | solution.py:56
  1.8 2.4 %collective-permute-start.3 = (f32[3,8,8,128]{3,2,1,0:T(8,128)S(1)}, f32[3,8,8,128]{3,2,1,0:T(8,128)S(1)}, u32[]{:S(2)}, u32[]{:S(2)}) collective-permute-start(f32[3,8,8,128]{3,2,1,0:T(8,128)S(1)} %get-tuple-element.21), channel_id=1, source_target_pairs={{0,8},{2,10},{4,12},{6,14},{8,0},{10,2},{12,4},{14,6},{1,9},{3,11}... | collective-permute-start | bytes 294920 | tf_op jit(solution)/shard_map/ppermute | solution.py:271
  4.2 1.2 %collective-permute-start = (f32[8,8,8,128]{3,2,1,0:T(8,128)S(1)}, f32[8,8,8,128]{3,2,1,0:T(8,128)S(1)}, u32[]{:S(2)}, u32[]{:S(2)}) collective-permute-start(f32[8,8,8,128]{3,2,1,0:T(8,128)S(1)} %get-tuple-element.18), channel_id=1, source_target_pairs={{0,2},{2,0},{4,6},{6,4},{8,10},{10,8},{12,14},{14,12},{1,3},{3,1},... | collective-permute-start | bytes 786440 | tf_op jit(solution)/shard_map/ppermute | solution.py:271
  5.5 0.2 collective-permute-start.1
  5.6 1.2 %collective-permute-start.2 = (f32[8,8,8,128]{3,2,1,0:T(8,128)S(1)}, f32[8,8,8,128]{3,2,1,0:T(8,128)S(1)}, u32[]{:S(2)}, u32[]{:S(2)}) collective-permute-start(f32[8,8,8,128]{3,2,1,0:T(8,128)S(1)} %get-tuple-element.20), channel_id=1, source_target_pairs={{0,6},{2,4},{4,2},{6,0},{8,14},{10,12},{12,10},{14,8},{1,7},{3,5},... | collective-permute-start | bytes 786440 | tf_op jit(solution)/shard_map/ppermute | solution.py:271
  6.9 1.0 %collective-permute-start.4 = (f32[8,8,8,128]{3,2,1,0:T(8,128)S(1)}, f32[8,8,8,128]{3,2,1,0:T(8,128)S(1)}, u32[]{:S(2)}, u32[]{:S(2)}) collective-permute-start(f32[8,8,8,128]{3,2,1,0:T(8,128)S(1)} %get-tuple-element.22), channel_id=1, source_target_pairs={{0,10},{2,8},{4,14},{6,12},{8,2},{10,0},{12,6},{14,4},{1,11},{3,9}... | collective-permute-start | bytes 786440 | tf_op jit(solution)/shard_map/ppermute | solution.py:271
  7.9 0.0 copy-done.1
  7.9 0.1 compare_convert_fusion
  8.0 0.0 copy-done
  8.0 0.6 %multiply_reduce_fusion = s32[8,4,8]{2,1,0:T(4,128)S(1)} fusion(s32[64,4,8]{0,2,1:T(8,128)S(1)} %constant_dynamic-slice_fusion, s32[8,64]{1,0:T(8,128)S(1)} %compare_convert_fusion), kind=kLoop, calls=%fused_computation | loop fusion | flops 32512 | bytes 11264 | tf_op jit(solution)/shard_map/reduce_sum | solution.py:249
  8.6 0.2 collective-permute-done.3.refs_1_
  8.8 1.2 %collective-permute-start.5 = (f32[8,8,8,128]{3,2,1,0:T(8,128)S(1)}, f32[8,8,8,128]{3,2,1,0:T(8,128)S(1)}, u32[]{:S(2)}, u32[]{:S(2)}) collective-permute-start(f32[8,8,8,128]{3,2,1,0:T(8,128)S(1)} %hand_on.3), channel_id=1, source_target_pairs={{0,12},{2,14},{4,8},{6,10},{8,4},{10,6},{12,0},{14,2},{1,13},{3,15... | collective-permute-start | bytes 786440 | tf_op jit(solution)/shard_map/ppermute | solution.py:271
  10.0 0.0 copy-done.2
  10.0 0.1 multiply_reduce_fusion.1
  10.1 0.1 copy.13
  10.2 14.2 %collective-permute-done.4.refs_2_.refs_1_ = f32[8,8,8,128]{3,2,1,0:T(8,128)S(1)} collective-permute-done((f32[8,8,8,128]{3,2,1,0:T(8,128)S(1)}, f32[8,8,8,128]{3,2,1,0:T(8,128)S(1)}, u32[]{:S(2)}, u32[]{:S(2)}) %collective-permute-start.4) | collective-permute-done | bytes 262176 | tf_op jit(solution)/shard_map/ppermute | solution.py:271
  24.4 2.7 %collective-permute-start.7 = (f32[3,8,8,128]{3,2,1,0:T(8,128)S(1)}, f32[3,8,8,128]{3,2,1,0:T(8,128)S(1)}, u32[]{:S(2)}, u32[]{:S(2)}) collective-permute-start(f32[3,8,8,128]{3,2,1,0:T(8,128)S(1)} %collective-permute-done.3.refs_1_), channel_id=1, source_target_pairs={{0,1},{1,0},{2,3},{3,2},{4,5},{5,4},{6,7},{7,6},{8,9},{9,8},{10,11... | collective-permute-start | bytes 294920 | tf_op jit(solution)/shard_map/ppermute | solution.py:263
  27.1 0.1 multiply_add_fusion
  27.2 0.1 add.28.bound_ref
  27.3 0.0 collective-permute-done.refs_1_
  27.3 0.1 collective-permute-start.10
  27.4 0.0 collective-permute-done.1.refs_2_
  27.4 0.0 collective-permute-done.2.refs_3_
  27.4 0.2 join_near.1.refs_0_
  27.6 0.1 collective-permute-start.6
  27.7 0.5 collective-permute-start.8
  28.2 0.0 collective-permute-done.5.refs_3_.refs_1_
  28.2 14.5 %collective-permute-start.11 = (f32[8,8,8,128]{3,2,1,0:T(8,128)S(1)}, f32[8,8,8,128]{3,2,1,0:T(8,128)S(1)}, u32[]{:S(2)}, u32[]{:S(2)}) collective-permute-start(f32[8,8,8,128]{3,2,1,0:T(8,128)S(1)} %hand_on.5), channel_id=1, source_target_pairs={{0,14},{2,12},{4,10},{6,8},{8,6},{10,4},{12,2},{14,0},{1,15},{3,13... | collective-permute-start | bytes 786440 | tf_op jit(solution)/shard_map/ppermute | solution.py:271
  42.7 0.0 collective-permute-done.7.refs_5_
  42.7 2.4 %collective-permute-start.9 = (f32[8,8,8,128]{3,2,1,0:T(8,128)S(1)}, f32[8,8,8,128]{3,2,1,0:T(8,128)S(1)}, u32[]{:S(2)}, u32[]{:S(2)}) collective-permute-start(f32[8,8,8,128]{3,2,1,0:T(8,128)S(1)} %collective-permute-done.5.refs_3_.refs_1_), channel_id=1, source_target_pairs={{0,1},{1,0},{2,3},{3,2},{4,5},{5,4},{6,7},{7,6},{8,9},{9,8},{10,11... | collective-permute-start | bytes 786440 | tf_op jit(solution)/shard_map/ppermute | solution.py:263
  45.1 6.5 %couple.1.refs_8_.matrix_ref = bf16[8,4,8,64,256]{4,3,2,1,0:T(8,128)(2,1)S(1)} custom-call(s32[256]{0:T(256)S(1)} %add.28.bound_ref, f32[8,4,8,64,128]{4,3,2,1,0:T(8,128)} %factor_ref.1), custom_call_target="tpu_custom_call" | custom-call | flops 30000001024 | bytes 16777216 | tf_op jit(solution)/shard_map/couple/pallas_call | solution.py:168
  51.7 0.0 collective-permute-done.10.refs_0_
  51.7 0.1 collective-permute-start.12
  51.7 0.0 collective-permute-done.11.refs_1_
  51.8 0.5 collective-permute-start.13
  52.2 0.0 collective-permute-done.8.refs_6_
  52.2 0.0 collective-permute-done.9.refs_7_
  52.3 0.0 collective-permute-done.6.refs_4_
  52.3 0.3 lay_rows.1
  52.6 0.5 collective-permute-done.12.refs_2_
  53.1 0.4 collective-permute-done.13.refs_3_
  53.5 4.6 %butterfly.1 = (f32[8,8,64,128]{3,2,1,0:T(8,128)}, f32[8,8,64,128]{3,2,1,0:T(8,128)S(1)}, f32[8,8,64,128]{3,2,1,0:T(8,128)S(1)}) custom-call(bf16[8,4,8,64,256]{4,3,2,1,0:T(8,128)(2,1)S(1)} %couple.1.refs_8_.matrix_ref, f32[8,8,64,128]{3,2,1,0:T(8,128)S(1)} %get-tuple-element.24.own_ref, ...), custom_call_target="tpu_custom_call", output_to_operand_aliasing={{1}: (1, {}), {2}: (2, {})} | custom-call | tf_op jit(solution)/shard_map/butterfly/pallas_call | solution.py:227
  (5 shorter events, 0.0 us)
Async XLA Ops:
  0.0 8.0 %copy-start = (s32[64,4,16]{0,2,1:T(8,128)S(1)}, s32[64,4,16]{0,2,1:T(8,128)}, u32[]{:S(2)}) copy-start(s32[64,4,16]{0,2,1:T(8,128)} %param.9) | copy-start | bytes 49156
  0.0 7.9 %copy-start.1 = (s32[64]{0:T(128)S(1)}, s32[64]{0:T(128)}, u32[]{:S(2)}) copy-start(s32[64]{0:T(128)} %slot_ref.1) | copy-start | bytes 772
  0.0 10.0 %copy-start.2 = (s32[64,4]{0,1:T(4,128)S(1)}, s32[64,4]{0,1:T(4,128)}, u32[]{:S(2)}) copy-start(s32[64,4]{0,1:T(4,128)} %param.8) | copy-start | bytes 3076
  1.8 6.9 %collective-permute-start.3 = (f32[3,8,8,128]{3,2,1,0:T(8,128)S(1)}, f32[3,8,8,128]{3,2,1,0:T(8,128)S(1)}, u32[]{:S(2)}, u32[]{:S(2)}) collective-permute-start(f32[3,8,8,128]{3,2,1,0:T(8,128)S(1)} %get-tuple-element.21), channel_id=1, source_target_pairs={{0,8},{2,10},{4,12},{6,14},{8,0},{10,2},{12,4},{14,6},{1,9},{3,11}... | collective-permute-start | bytes 294920 | tf_op jit(solution)/shard_map/ppermute | solution.py:271
  4.2 23.1 %collective-permute-start = (f32[8,8,8,128]{3,2,1,0:T(8,128)S(1)}, f32[8,8,8,128]{3,2,1,0:T(8,128)S(1)}, u32[]{:S(2)}, u32[]{:S(2)}) collective-permute-start(f32[8,8,8,128]{3,2,1,0:T(8,128)S(1)} %get-tuple-element.18), channel_id=1, source_target_pairs={{0,2},{2,0},{4,6},{6,4},{8,10},{10,8},{12,14},{14,12},{1,3},{3,1},... | collective-permute-start | bytes 786440 | tf_op jit(solution)/shard_map/ppermute | solution.py:271
  5.5 21.9 %collective-permute-start.1 = (f32[8,8,8,128]{3,2,1,0:T(8,128)S(1)}, f32[8,8,8,128]{3,2,1,0:T(8,128)S(1)}, u32[]{:S(2)}, u32[]{:S(2)}) collective-permute-start(f32[8,8,8,128]{3,2,1,0:T(8,128)S(1)} %get-tuple-element.19), channel_id=1, source_target_pairs={{0,4},{2,6},{4,0},{6,2},{8,12},{10,14},{12,8},{14,10},{1,5},{3,7},... | collective-permute-start | bytes 786440 | tf_op jit(solution)/shard_map/ppermute | solution.py:271
  5.6 21.8 %collective-permute-start.2 = (f32[8,8,8,128]{3,2,1,0:T(8,128)S(1)}, f32[8,8,8,128]{3,2,1,0:T(8,128)S(1)}, u32[]{:S(2)}, u32[]{:S(2)}) collective-permute-start(f32[8,8,8,128]{3,2,1,0:T(8,128)S(1)} %get-tuple-element.20), channel_id=1, source_target_pairs={{0,6},{2,4},{4,2},{6,0},{8,14},{10,12},{12,10},{14,8},{1,7},{3,5},... | collective-permute-start | bytes 786440 | tf_op jit(solution)/shard_map/ppermute | solution.py:271
  6.9 17.5 %collective-permute-start.4 = (f32[8,8,8,128]{3,2,1,0:T(8,128)S(1)}, f32[8,8,8,128]{3,2,1,0:T(8,128)S(1)}, u32[]{:S(2)}, u32[]{:S(2)}) collective-permute-start(f32[8,8,8,128]{3,2,1,0:T(8,128)S(1)} %get-tuple-element.22), channel_id=1, source_target_pairs={{0,10},{2,8},{4,14},{6,12},{8,2},{10,0},{12,6},{14,4},{1,11},{3,9}... | collective-permute-start | bytes 786440 | tf_op jit(solution)/shard_map/ppermute | solution.py:271
  8.8 19.4 %collective-permute-start.5 = (f32[8,8,8,128]{3,2,1,0:T(8,128)S(1)}, f32[8,8,8,128]{3,2,1,0:T(8,128)S(1)}, u32[]{:S(2)}, u32[]{:S(2)}) collective-permute-start(f32[8,8,8,128]{3,2,1,0:T(8,128)S(1)} %hand_on.3), channel_id=1, source_target_pairs={{0,12},{2,14},{4,8},{6,10},{8,4},{10,6},{12,0},{14,2},{1,13},{3,15... | collective-permute-start | bytes 786440 | tf_op jit(solution)/shard_map/ppermute | solution.py:271
  24.4 18.3 %collective-permute-start.7 = (f32[3,8,8,128]{3,2,1,0:T(8,128)S(1)}, f32[3,8,8,128]{3,2,1,0:T(8,128)S(1)}, u32[]{:S(2)}, u32[]{:S(2)}) collective-permute-start(f32[3,8,8,128]{3,2,1,0:T(8,128)S(1)} %collective-permute-done.3.refs_1_), channel_id=1, source_target_pairs={{0,1},{1,0},{2,3},{3,2},{4,5},{5,4},{6,7},{7,6},{8,9},{9,8},{10,11... | collective-permute-start | bytes 294920 | tf_op jit(solution)/shard_map/ppermute | solution.py:263
  27.3 24.3 %collective-permute-start.10 = (f32[5,8,8,128]{3,2,1,0:T(8,128)S(1)}, f32[5,8,8,128]{3,2,1,0:T(8,128)S(1)}, u32[]{:S(2)}, u32[]{:S(2)}) collective-permute-start(f32[5,8,8,128]{3,2,1,0:T(8,128)S(1)} %hand_on.4), channel_id=1, source_target_pairs={{0,8},{2,10},{4,12},{6,14},{8,0},{10,2},{12,4},{14,6},{1,9},{3,11}... | collective-permute-start | bytes 491528 | tf_op jit(solution)/shard_map/ppermute | solution.py:271
  27.6 24.7 %collective-permute-start.6 = (f32[8,8,32,128]{3,2,1,0:T(8,128)S(1)}, f32[8,8,32,128]{3,2,1,0:T(8,128)S(1)}, u32[]{:S(2)}, u32[]{:S(2)}) collective-permute-start(f32[8,8,32,128]{3,2,1,0:T(8,128)S(1)} %join_near.1.refs_0_), channel_id=1, source_target_pairs={{0,1},{1,0},{2,3},{3,2},{4,5},{5,4},{6,7},{7,6},{8,9},{9,8},{10,11... | collective-permute-start | bytes 3145736 | tf_op jit(solution)/shard_map/ppermute | solution.py:263
  27.7 24.6 %collective-permute-start.8 = (f32[8,8,8,128]{3,2,1,0:T(8,128)S(1)}, f32[8,8,8,128]{3,2,1,0:T(8,128)S(1)}, u32[]{:S(2)}, u32[]{:S(2)}) collective-permute-start(f32[8,8,8,128]{3,2,1,0:T(8,128)S(1)} %collective-permute-done.4.refs_2_.refs_1_), channel_id=1, source_target_pairs={{0,1},{1,0},{2,3},{3,2},{4,5},{5,4},{6,7},{7,6},{8,9},{9,8},{10,11... | collective-permute-start | bytes 786440 | tf_op jit(solution)/shard_map/ppermute | solution.py:263
  28.2 23.6 %collective-permute-start.11 = (f32[8,8,8,128]{3,2,1,0:T(8,128)S(1)}, f32[8,8,8,128]{3,2,1,0:T(8,128)S(1)}, u32[]{:S(2)}, u32[]{:S(2)}) collective-permute-start(f32[8,8,8,128]{3,2,1,0:T(8,128)S(1)} %hand_on.5), channel_id=1, source_target_pairs={{0,14},{2,12},{4,10},{6,8},{8,6},{10,4},{12,2},{14,0},{1,15},{3,13... | collective-permute-start | bytes 786440 | tf_op jit(solution)/shard_map/ppermute | solution.py:271
  42.7 9.5 %collective-permute-start.9 = (f32[8,8,8,128]{3,2,1,0:T(8,128)S(1)}, f32[8,8,8,128]{3,2,1,0:T(8,128)S(1)}, u32[]{:S(2)}, u32[]{:S(2)}) collective-permute-start(f32[8,8,8,128]{3,2,1,0:T(8,128)S(1)} %collective-permute-done.5.refs_3_.refs_1_), channel_id=1, source_target_pairs={{0,1},{1,0},{2,3},{3,2},{4,5},{5,4},{6,7},{7,6},{8,9},{9,8},{10,11... | collective-permute-start | bytes 786440 | tf_op jit(solution)/shard_map/ppermute | solution.py:263
  51.7 1.5 %collective-permute-start.12 = (f32[5,8,8,128]{3,2,1,0:T(8,128)S(1)}, f32[5,8,8,128]{3,2,1,0:T(8,128)S(1)}, u32[]{:S(2)}, u32[]{:S(2)}) collective-permute-start(f32[5,8,8,128]{3,2,1,0:T(8,128)S(1)} %collective-permute-done.10.refs_0_), channel_id=1, source_target_pairs={{0,1},{1,0},{2,3},{3,2},{4,5},{5,4},{6,7},{7,6},{8,9},{9,8},{10,11... | collective-permute-start | bytes 491528 | tf_op jit(solution)/shard_map/ppermute | solution.py:263
  51.8 1.7 %collective-permute-start.13 = (f32[8,8,8,128]{3,2,1,0:T(8,128)S(1)}, f32[8,8,8,128]{3,2,1,0:T(8,128)S(1)}, u32[]{:S(2)}, u32[]{:S(2)}) collective-permute-start(f32[8,8,8,128]{3,2,1,0:T(8,128)S(1)} %collective-permute-done.11.refs_1_), channel_id=1, source_target_pairs={{0,1},{1,0},{2,3},{3,2},{4,5},{5,4},{6,7},{7,6},{8,9},{9,8},{10,11... | collective-permute-start | bytes 786440 | tf_op jit(solution)/shard_map/ppermute | solution.py:263

commit v4 on v3

--- a/solution.py
+++ b/solution.py
@@ -192,48 +192,46 @@
 
 
 def butterfly_kernel(steps, matrix_ref, own_ref, partner_ref, *refs):
-    pieces, out_ref = refs[: 2 * len(steps)], refs[2 * len(steps)]
-    own, partner = refs[-2:]
-    _, levels, blocks, rows, _ = matrix_ref.shape
-    together = out_ref.shape[0]
-
-    @pl.when(pl.program_id(0) == 0)
-    def _():
-        place(own, steps, pieces[: len(steps)])
-        place(partner, steps, pieces[len(steps) :])
-
-    slots = [pl.program_id(0) * together + t for t in range(together)]
-    for i in range(blocks):
-        for t, slot in enumerate(slots):
-            out_ref[t, i] = product(matrix_ref[slot, 0, i], own[slot, i], partner[slot, i])
-    for level in range(1, levels):
-        dist = blocks >> level
+    pieces, (out_ref, own, partner, state, sems) = refs[: 2 * len(steps)], refs[-5:]
+    slot_count, levels, blocks, rows, _ = matrix_ref.shape
+    place(own, steps, pieces[: len(steps)])
+    place(partner, steps, pieces[len(steps) :])
+
+    def pair(level, i, slot):
+        j = i ^ (blocks >> level)
+        if i < j:
+            matrix = jnp.concatenate([matrix_ref[slot, level, i], matrix_ref[slot, level, j]], axis=0)
+            both = product(matrix, state[slot, i], state[slot, j])
+            state[slot, i], state[slot, j] = both[:rows], both[rows:]
+
+    copies = []
+    for low in range(0, slot_count, TOGETHER):
+        slots = range(low, min(low + TOGETHER, slot_count))
         for i in range(blocks):
-            for t, slot in enumerate(slots):
-                j = i ^ dist
-                if i < j:
-                    matrix = jnp.concatenate(
-                        [matrix_ref[slot, level, i], matrix_ref[slot, level, j]], axis=0
-                    )
-                    both = product(matrix, out_ref[t, i], out_ref[t, j])
-                    out_ref[t, i], out_ref[t, j] = both[:rows], both[rows:]
+            for slot in slots:
+                state[slot, i] = product(matrix_ref[slot, 0, i], own[slot, i], partner[slot, i])
+        for level in range(1, levels - 1):
+            for i in range(blocks):
+                for slot in slots:
+                    pair(level, i, slot)
+        for slot in slots:
+            for i in range(blocks):
+                pair(levels - 1, i, slot)
+            copies.append(pltpu.make_async_copy(state.at[slot], out_ref.at[slot], sems.at[slot]))
+            copies[-1].start()
+    for copy in copies:
+        copy.wait()
 
 
 def butterfly(steps, matrices, own, partner, own_pieces, partner_pieces):
-    count, blocks, rows, columns = own.shape
     args = [matrices, own, partner] + own_pieces + partner_pieces
     state = pltpu.VMEM(own.shape, own.dtype)
-    together = max(t for t in range(1, TOGETHER + 1) if count % t == 0)
     return pl.pallas_call(
         functools.partial(butterfly_kernel, steps),
-        grid=(count // together,),
-        out_shape=[jax.ShapeDtypeStruct(own.shape, own.dtype), state, state],
+        out_shape=[pltpu.HBM(own.shape, own.dtype), state, state],
         in_specs=[VMEM] * len(args),
-        out_specs=[
-            pl.BlockSpec((together, blocks, rows, columns), lambda s: (s, 0, 0, 0)),
-            VMEM,
-            VMEM,
-        ],
+        out_specs=[ANY, VMEM, VMEM],
+        scratch_shapes=[state, pltpu.SemaphoreType.DMA((own.shape[0],))],
         input_output_aliases={1: 1, 2: 2},
         compiler_params=pltpu.CompilerParams(vmem_limit_bytes=12 * 1024 * 1024),
         cost_estimate=pl.CostEstimate(flops=0, bytes_accessed=0, transcendentals=0),

time: 58.4 us -> 58 us (level)
  no operation moved by 1% of the time
where the time goes in v4:
time: 58 us; the launch traced here: 57.7 us
  starting transfers between devices  28.2 us (49%)
  waiting for transfers between devices  15.3 us (26%)
  Pallas kernels  13.1 us (23%)
  other arithmetic  0.92 us (2%)
    ppermute x8, starting transfers between devices, hop(): return lax.ppermute(piece, 'order', [(g, g ^ k) for g in range(groups)])  21.9 us
    ppermute x8, waiting for transfers between devices, hop(): return lax.ppermute(piece, 'order', [(g, g ^ k) for g in range(groups)])  14.3 us
    pallas_call x1, Pallas kernels, couple(): pl.pallas_call(couple_kernel, grid=(slot_count,), out_shape=pltpu.VMEM((s...  6.52 us
    ppermute x6, starting transfers between devices, over(): return lax.ppermute(piece, 'lat', swap)  6.3 us
    pallas_call x1, Pallas kernels, butterfly(): pl.pallas_call(functools.partial(butterfly_kernel, steps), out_shape=[plt...  4.25 us
    pallas_call x1, Pallas kernels, gather(): pl.pallas_call(functools.partial(gather_kernel, plan, slot_count), out_sh...  1.83 us
  transfers between devices with their start and end apart: 14, of which 4 were waited for; matrix products, arithmetic and copies ran while one was open for 2% of the time, Pallas kernels for 12%

profile of v4, /device:TPU:9, one launch (start us, length us, event | category | flops | bytes accessed | tf_op | source)
XLA Modules:
  0.0 57.7 jit_solution(15843988104772704988)
XLA Ops:
  0.0 0.0 copy-start
  0.0 0.0 copy-start.1
  0.0 0.0 copy-start.2
  0.0 1.8 %gather_rows.1 = (f32[8,8,8,128]{3,2,1,0:T(8,128)S(1)}, f32[8,8,8,128]{3,2,1,0:T(8,128)S(1)}, f32[8,8,8,128]{3,2,1,0:T(8,128)S(1)}, f32[8,8,8,128]{3,2,1,0:T(8,1...) custom-call(s32[64]{0:T(128)} %slot_ref.1, ...), custom_call_target="tpu_custom_call" | custom-call | bytes 4194304 | tf_op jit(solution)/shard_map/gather_rows/pallas_call | solution.py:56
  1.8 2.4 %collective-permute-start.3 = (f32[3,8,8,128]{3,2,1,0:T(8,128)S(1)}, f32[3,8,8,128]{3,2,1,0:T(8,128)S(1)}, u32[]{:S(2)}, u32[]{:S(2)}) collective-permute-start(f32[3,8,8,128]{3,2,1,0:T(8,128)S(1)} %get-tuple-element.21), channel_id=1, source_target_pairs={{0,8},{2,10},{4,12},{6,14},{8,0},{10,2},{12,4},{14,6},{1,9},{3,11}... | collective-permute-start | bytes 294920 | tf_op jit(solution)/shard_map/ppermute | solution.py:269
  4.2 1.2 %collective-permute-start = (f32[8,8,8,128]{3,2,1,0:T(8,128)S(1)}, f32[8,8,8,128]{3,2,1,0:T(8,128)S(1)}, u32[]{:S(2)}, u32[]{:S(2)}) collective-permute-start(f32[8,8,8,128]{3,2,1,0:T(8,128)S(1)} %get-tuple-element.18), channel_id=1, source_target_pairs={{0,2},{2,0},{4,6},{6,4},{8,10},{10,8},{12,14},{14,12},{1,3},{3,1},... | collective-permute-start | bytes 786440 | tf_op jit(solution)/shard_map/ppermute | solution.py:269
  5.5 0.2 collective-permute-start.1
  5.6 1.2 %collective-permute-start.2 = (f32[8,8,8,128]{3,2,1,0:T(8,128)S(1)}, f32[8,8,8,128]{3,2,1,0:T(8,128)S(1)}, u32[]{:S(2)}, u32[]{:S(2)}) collective-permute-start(f32[8,8,8,128]{3,2,1,0:T(8,128)S(1)} %get-tuple-element.20), channel_id=1, source_target_pairs={{0,6},{2,4},{4,2},{6,0},{8,14},{10,12},{12,10},{14,8},{1,7},{3,5},... | collective-permute-start | bytes 786440 | tf_op jit(solution)/shard_map/ppermute | solution.py:269
  6.9 1.0 %collective-permute-start.4 = (f32[8,8,8,128]{3,2,1,0:T(8,128)S(1)}, f32[8,8,8,128]{3,2,1,0:T(8,128)S(1)}, u32[]{:S(2)}, u32[]{:S(2)}) collective-permute-start(f32[8,8,8,128]{3,2,1,0:T(8,128)S(1)} %get-tuple-element.22), channel_id=1, source_target_pairs={{0,10},{2,8},{4,14},{6,12},{8,2},{10,0},{12,6},{14,4},{1,11},{3,9}... | collective-permute-start | bytes 786440 | tf_op jit(solution)/shard_map/ppermute | solution.py:269
  7.9 0.0 copy-done.1
  7.9 0.1 compare_convert_fusion
  8.0 0.0 copy-done
  8.0 0.6 %multiply_reduce_fusion = s32[8,4,8]{2,1,0:T(4,128)S(1)} fusion(s32[64,4,8]{0,2,1:T(8,128)S(1)} %constant_dynamic-slice_fusion, s32[8,64]{1,0:T(8,128)S(1)} %compare_convert_fusion), kind=kLoop, calls=%fused_computation | loop fusion | flops 32512 | bytes 11264 | tf_op jit(solution)/shard_map/reduce_sum | solution.py:247
  8.6 0.2 collective-permute-done.3.refs_1_
  8.8 1.2 %collective-permute-start.5 = (f32[8,8,8,128]{3,2,1,0:T(8,128)S(1)}, f32[8,8,8,128]{3,2,1,0:T(8,128)S(1)}, u32[]{:S(2)}, u32[]{:S(2)}) collective-permute-start(f32[8,8,8,128]{3,2,1,0:T(8,128)S(1)} %hand_on.3), channel_id=1, source_target_pairs={{0,12},{2,14},{4,8},{6,10},{8,4},{10,6},{12,0},{14,2},{1,13},{3,15... | collective-permute-start | bytes 786440 | tf_op jit(solution)/shard_map/ppermute | solution.py:269
  10.0 0.0 copy-done.2
  10.0 0.1 multiply_reduce_fusion.1
  10.1 0.1 copy.13
  10.2 14.2 %collective-permute-done.4.refs_2_.refs_1_ = f32[8,8,8,128]{3,2,1,0:T(8,128)S(1)} collective-permute-done((f32[8,8,8,128]{3,2,1,0:T(8,128)S(1)}, f32[8,8,8,128]{3,2,1,0:T(8,128)S(1)}, u32[]{:S(2)}, u32[]{:S(2)}) %collective-permute-start.4) | collective-permute-done | bytes 262176 | tf_op jit(solution)/shard_map/ppermute | solution.py:269
  24.4 2.7 %collective-permute-start.7 = (f32[3,8,8,128]{3,2,1,0:T(8,128)S(1)}, f32[3,8,8,128]{3,2,1,0:T(8,128)S(1)}, u32[]{:S(2)}, u32[]{:S(2)}) collective-permute-start(f32[3,8,8,128]{3,2,1,0:T(8,128)S(1)} %collective-permute-done.3.refs_1_), channel_id=1, source_target_pairs={{0,1},{1,0},{2,3},{3,2},{4,5},{5,4},{6,7},{7,6},{8,9},{9,8},{10,11... | collective-permute-start | bytes 294920 | tf_op jit(solution)/shard_map/ppermute | solution.py:261
  27.1 0.1 multiply_add_fusion
  27.2 0.1 add.28.bound_ref
  27.3 0.0 collective-permute-done.refs_1_
  27.3 0.1 collective-permute-start.10
  27.4 0.0 collective-permute-done.1.refs_2_
  27.4 0.0 collective-permute-done.2.refs_3_
  27.4 0.2 join_near.1.refs_0_
  27.6 0.1 collective-permute-start.6
  27.7 0.5 collective-permute-start.8
  28.2 0.0 collective-permute-done.5.refs_3_.refs_1_
  28.2 14.5 %collective-permute-start.11 = (f32[8,8,8,128]{3,2,1,0:T(8,128)S(1)}, f32[8,8,8,128]{3,2,1,0:T(8,128)S(1)}, u32[]{:S(2)}, u32[]{:S(2)}) collective-permute-start(f32[8,8,8,128]{3,2,1,0:T(8,128)S(1)} %hand_on.5), channel_id=1, source_target_pairs={{0,14},{2,12},{4,10},{6,8},{8,6},{10,4},{12,2},{14,0},{1,15},{3,13... | collective-permute-start | bytes 786440 | tf_op jit(solution)/shard_map/ppermute | solution.py:269
  42.7 0.0 collective-permute-done.7.refs_5_
  42.7 2.4 %collective-permute-start.9 = (f32[8,8,8,128]{3,2,1,0:T(8,128)S(1)}, f32[8,8,8,128]{3,2,1,0:T(8,128)S(1)}, u32[]{:S(2)}, u32[]{:S(2)}) collective-permute-start(f32[8,8,8,128]{3,2,1,0:T(8,128)S(1)} %collective-permute-done.5.refs_3_.refs_1_), channel_id=1, source_target_pairs={{0,1},{1,0},{2,3},{3,2},{4,5},{5,4},{6,7},{7,6},{8,9},{9,8},{10,11... | collective-permute-start | bytes 786440 | tf_op jit(solution)/shard_map/ppermute | solution.py:261
  45.1 6.5 %couple.1.refs_8_.matrix_ref = bf16[8,4,8,64,256]{4,3,2,1,0:T(8,128)(2,1)S(1)} custom-call(s32[256]{0:T(256)S(1)} %add.28.bound_ref, f32[8,4,8,64,128]{4,3,2,1,0:T(8,128)} %factor_ref.1), custom_call_target="tpu_custom_call" | custom-call | flops 30000001024 | bytes 16777216 | tf_op jit(solution)/shard_map/couple/pallas_call | solution.py:168
  51.7 0.0 collective-permute-done.10.refs_0_
  51.7 0.1 collective-permute-start.12
  51.7 0.0 collective-permute-done.11.refs_1_
  51.8 0.5 collective-permute-start.13
  52.2 0.0 collective-permute-done.8.refs_6_
  52.2 0.0 collective-permute-done.9.refs_7_
  52.3 0.0 collective-permute-done.6.refs_4_
  52.3 0.3 lay_rows.1
  52.6 0.5 collective-permute-done.12.refs_2_
  53.1 0.4 collective-permute-done.13.refs_3_
  53.5 4.2 %butterfly.1 = (f32[8,8,64,128]{3,2,1,0:T(8,128)}, f32[8,8,64,128]{3,2,1,0:T(8,128)S(1)}, f32[8,8,64,128]{3,2,1,0:T(8,128)S(1)}) custom-call(bf16[8,4,8,64,256]{4,3,2,1,0:T(8,128)(2,1)S(1)} %couple.1.refs_8_.matrix_ref, f32[8,8,64,128]{3,2,1,0:T(8,128)S(1)} %get-tuple-element.24.own_ref, ...), custom_call_target="tpu_custom_call", output_to_operand_aliasing={{1}: (1, {}), {2}: (2, {})} | custom-call | tf_op jit(solution)/shard_map/butterfly/pallas_call | solution.py:229
  (5 shorter events, 0.0 us)
Async XLA Ops:
  0.0 8.0 %copy-start = (s32[64,4,16]{0,2,1:T(8,128)S(1)}, s32[64,4,16]{0,2,1:T(8,128)}, u32[]{:S(2)}) copy-start(s32[64,4,16]{0,2,1:T(8,128)} %param.9) | copy-start | bytes 49156
  0.0 7.9 %copy-start.1 = (s32[64]{0:T(128)S(1)}, s32[64]{0:T(128)}, u32[]{:S(2)}) copy-start(s32[64]{0:T(128)} %slot_ref.1) | copy-start | bytes 772
  0.0 10.0 %copy-start.2 = (s32[64,4]{0,1:T(4,128)S(1)}, s32[64,4]{0,1:T(4,128)}, u32[]{:S(2)}) copy-start(s32[64,4]{0,1:T(4,128)} %param.8) | copy-start | bytes 3076
  1.8 6.9 %collective-permute-start.3 = (f32[3,8,8,128]{3,2,1,0:T(8,128)S(1)}, f32[3,8,8,128]{3,2,1,0:T(8,128)S(1)}, u32[]{:S(2)}, u32[]{:S(2)}) collective-permute-start(f32[3,8,8,128]{3,2,1,0:T(8,128)S(1)} %get-tuple-element.21), channel_id=1, source_target_pairs={{0,8},{2,10},{4,12},{6,14},{8,0},{10,2},{12,4},{14,6},{1,9},{3,11}... | collective-permute-start | bytes 294920 | tf_op jit(solution)/shard_map/ppermute | solution.py:269
  4.2 23.1 %collective-permute-start = (f32[8,8,8,128]{3,2,1,0:T(8,128)S(1)}, f32[8,8,8,128]{3,2,1,0:T(8,128)S(1)}, u32[]{:S(2)}, u32[]{:S(2)}) collective-permute-start(f32[8,8,8,128]{3,2,1,0:T(8,128)S(1)} %get-tuple-element.18), channel_id=1, source_target_pairs={{0,2},{2,0},{4,6},{6,4},{8,10},{10,8},{12,14},{14,12},{1,3},{3,1},... | collective-permute-start | bytes 786440 | tf_op jit(solution)/shard_map/ppermute | solution.py:269
  5.5 21.9 %collective-permute-start.1 = (f32[8,8,8,128]{3,2,1,0:T(8,128)S(1)}, f32[8,8,8,128]{3,2,1,0:T(8,128)S(1)}, u32[]{:S(2)}, u32[]{:S(2)}) collective-permute-start(f32[8,8,8,128]{3,2,1,0:T(8,128)S(1)} %get-tuple-element.19), channel_id=1, source_target_pairs={{0,4},{2,6},{4,0},{6,2},{8,12},{10,14},{12,8},{14,10},{1,5},{3,7},... | collective-permute-start | bytes 786440 | tf_op jit(solution)/shard_map/ppermute | solution.py:269
  5.6 21.8 %collective-permute-start.2 = (f32[8,8,8,128]{3,2,1,0:T(8,128)S(1)}, f32[8,8,8,128]{3,2,1,0:T(8,128)S(1)}, u32[]{:S(2)}, u32[]{:S(2)}) collective-permute-start(f32[8,8,8,128]{3,2,1,0:T(8,128)S(1)} %get-tuple-element.20), channel_id=1, source_target_pairs={{0,6},{2,4},{4,2},{6,0},{8,14},{10,12},{12,10},{14,8},{1,7},{3,5},... | collective-permute-start | bytes 786440 | tf_op jit(solution)/shard_map/ppermute | solution.py:269
  6.9 17.5 %collective-permute-start.4 = (f32[8,8,8,128]{3,2,1,0:T(8,128)S(1)}, f32[8,8,8,128]{3,2,1,0:T(8,128)S(1)}, u32[]{:S(2)}, u32[]{:S(2)}) collective-permute-start(f32[8,8,8,128]{3,2,1,0:T(8,128)S(1)} %get-tuple-element.22), channel_id=1, source_target_pairs={{0,10},{2,8},{4,14},{6,12},{8,2},{10,0},{12,6},{14,4},{1,11},{3,9}... | collective-permute-start | bytes 786440 | tf_op jit(solution)/shard_map/ppermute | solution.py:269
  8.8 19.4 %collective-permute-start.5 = (f32[8,8,8,128]{3,2,1,0:T(8,128)S(1)}, f32[8,8,8,128]{3,2,1,0:T(8,128)S(1)}, u32[]{:S(2)}, u32[]{:S(2)}) collective-permute-start(f32[8,8,8,128]{3,2,1,0:T(8,128)S(1)} %hand_on.3), channel_id=1, source_target_pairs={{0,12},{2,14},{4,8},{6,10},{8,4},{10,6},{12,0},{14,2},{1,13},{3,15... | collective-permute-start | bytes 786440 | tf_op jit(solution)/shard_map/ppermute | solution.py:269
  24.4 18.3 %collective-permute-start.7 = (f32[3,8,8,128]{3,2,1,0:T(8,128)S(1)}, f32[3,8,8,128]{3,2,1,0:T(8,128)S(1)}, u32[]{:S(2)}, u32[]{:S(2)}) collective-permute-start(f32[3,8,8,128]{3,2,1,0:T(8,128)S(1)} %collective-permute-done.3.refs_1_), channel_id=1, source_target_pairs={{0,1},{1,0},{2,3},{3,2},{4,5},{5,4},{6,7},{7,6},{8,9},{9,8},{10,11... | collective-permute-start | bytes 294920 | tf_op jit(solution)/shard_map/ppermute | solution.py:261
  27.3 24.3 %collective-permute-start.10 = (f32[5,8,8,128]{3,2,1,0:T(8,128)S(1)}, f32[5,8,8,128]{3,2,1,0:T(8,128)S(1)}, u32[]{:S(2)}, u32[]{:S(2)}) collective-permute-start(f32[5,8,8,128]{3,2,1,0:T(8,128)S(1)} %hand_on.4), channel_id=1, source_target_pairs={{0,8},{2,10},{4,12},{6,14},{8,0},{10,2},{12,4},{14,6},{1,9},{3,11}... | collective-permute-start | bytes 491528 | tf_op jit(solution)/shard_map/ppermute | solution.py:269
  27.6 24.7 %collective-permute-start.6 = (f32[8,8,32,128]{3,2,1,0:T(8,128)S(1)}, f32[8,8,32,128]{3,2,1,0:T(8,128)S(1)}, u32[]{:S(2)}, u32[]{:S(2)}) collective-permute-start(f32[8,8,32,128]{3,2,1,0:T(8,128)S(1)} %join_near.1.refs_0_), channel_id=1, source_target_pairs={{0,1},{1,0},{2,3},{3,2},{4,5},{5,4},{6,7},{7,6},{8,9},{9,8},{10,11... | collective-permute-start | bytes 3145736 | tf_op jit(solution)/shard_map/ppermute | solution.py:261
  27.7 24.6 %collective-permute-start.8 = (f32[8,8,8,128]{3,2,1,0:T(8,128)S(1)}, f32[8,8,8,128]{3,2,1,0:T(8,128)S(1)}, u32[]{:S(2)}, u32[]{:S(2)}) collective-permute-start(f32[8,8,8,128]{3,2,1,0:T(8,128)S(1)} %collective-permute-done.4.refs_2_.refs_1_), channel_id=1, source_target_pairs={{0,1},{1,0},{2,3},{3,2},{4,5},{5,4},{6,7},{7,6},{8,9},{9,8},{10,11... | collective-permute-start | bytes 786440 | tf_op jit(solution)/shard_map/ppermute | solution.py:261
  28.2 23.6 %collective-permute-start.11 = (f32[8,8,8,128]{3,2,1,0:T(8,128)S(1)}, f32[8,8,8,128]{3,2,1,0:T(8,128)S(1)}, u32[]{:S(2)}, u32[]{:S(2)}) collective-permute-start(f32[8,8,8,128]{3,2,1,0:T(8,128)S(1)} %hand_on.5), channel_id=1, source_target_pairs={{0,14},{2,12},{4,10},{6,8},{8,6},{10,4},{12,2},{14,0},{1,15},{3,13... | collective-permute-start | bytes 786440 | tf_op jit(solution)/shard_map/ppermute | solution.py:269
  42.7 9.5 %collective-permute-start.9 = (f32[8,8,8,128]{3,2,1,0:T(8,128)S(1)}, f32[8,8,8,128]{3,2,1,0:T(8,128)S(1)}, u32[]{:S(2)}, u32[]{:S(2)}) collective-permute-start(f32[8,8,8,128]{3,2,1,0:T(8,128)S(1)} %collective-permute-done.5.refs_3_.refs_1_), channel_id=1, source_target_pairs={{0,1},{1,0},{2,3},{3,2},{4,5},{5,4},{6,7},{7,6},{8,9},{9,8},{10,11... | collective-permute-start | bytes 786440 | tf_op jit(solution)/shard_map/ppermute | solution.py:261
  51.7 1.5 %collective-permute-start.12 = (f32[5,8,8,128]{3,2,1,0:T(8,128)S(1)}, f32[5,8,8,128]{3,2,1,0:T(8,128)S(1)}, u32[]{:S(2)}, u32[]{:S(2)}) collective-permute-start(f32[5,8,8,128]{3,2,1,0:T(8,128)S(1)} %collective-permute-done.10.refs_0_), channel_id=1, source_target_pairs={{0,1},{1,0},{2,3},{3,2},{4,5},{5,4},{6,7},{7,6},{8,9},{9,8},{10,11... | collective-permute-start | bytes 491528 | tf_op jit(solution)/shard_map/ppermute | solution.py:261
  51.8 1.7 %collective-permute-start.13 = (f32[8,8,8,128]{3,2,1,0:T(8,128)S(1)}, f32[8,8,8,128]{3,2,1,0:T(8,128)S(1)}, u32[]{:S(2)}, u32[]{:S(2)}) collective-permute-start(f32[8,8,8,128]{3,2,1,0:T(8,128)S(1)} %collective-permute-done.11.refs_1_), channel_id=1, source_target_pairs={{0,1},{1,0},{2,3},{3,2},{4,5},{5,4},{6,7},{7,6},{8,9},{9,8},{10,11... | collective-permute-start | bytes 786440 | tf_op jit(solution)/shard_map/ppermute | solution.py:261

commit v5 on v4

--- a/solution.py
+++ b/solution.py
@@ -268,7 +268,7 @@
     def hop(piece, k):
         return lax.ppermute(piece, "order", [(g, g ^ k) for g in range(groups)])
 
-    half, head = groups // 2, max(1, 3 * slot_count // 8)
+    half, head = groups // 2, max(1, slot_count // 2)
     near = [(k, 0, slot_count) for k in range(half)]
     far = [
         ((half, 0, head), None),

time: 58 us -> 57.9 us (level)
  starting transfers between devices: 28.2 us -> 19.9 us
  waiting for transfers between devices: 15.3 us -> 23.4 us
    ppermute x8, waiting for transfers between devices: 14.3 us -> 22.6 us  [hop(): return lax.ppermute(piece, 'order', [(g, g ^ k) for g in range(groups)])]
    ppermute x8, starting transfers between devices: 21.9 us -> 15.2 us  [hop(): return lax.ppermute(piece, 'order', [(g, g ^ k) for g in range(groups)])]
    ppermute x6, starting transfers between devices: 6.3 us -> 4.66 us  [over(): return lax.ppermute(piece, 'lat', swap)]
  transfers between devices with their start and end apart: 14 -> 14, of which waited for: 4 -> 5; matrix products, arithmetic and copies ran while one was open for 2% -> 2% of each run, Pallas kernels for 12% -> 12%
where the time goes in v5:
time: 57.9 us; the launch traced here: 57.7 us
  waiting for transfers between devices  23.4 us (40%)
  starting transfers between devices  19.9 us (34%)
  Pallas kernels  13.1 us (23%)
  other arithmetic  0.92 us (2%)
    ppermute x8, waiting for transfers between devices, hop(): return lax.ppermute(piece, 'order', [(g, g ^ k) for g in range(groups)])  22.6 us
    ppermute x8, starting transfers between devices, hop(): return lax.ppermute(piece, 'order', [(g, g ^ k) for g in range(groups)])  15.2 us
    pallas_call x1, Pallas kernels, couple(): pl.pallas_call(couple_kernel, grid=(slot_count,), out_shape=pltpu.VMEM((s...  6.52 us
    ppermute x6, starting transfers between devices, over(): return lax.ppermute(piece, 'lat', swap)  4.66 us
    pallas_call x1, Pallas kernels, butterfly(): pl.pallas_call(functools.partial(butterfly_kernel, steps), out_shape=[plt...  4.24 us
    pallas_call x1, Pallas kernels, gather(): pl.pallas_call(functools.partial(gather_kernel, plan, slot_count), out_sh...  1.83 us
  transfers between devices with their start and end apart: 14, of which 5 were waited for; matrix products, arithmetic and copies ran while one was open for 2% of the time, Pallas kernels for 12%

profile of v5, /device:TPU:9, one launch (start us, length us, event | category | flops | bytes accessed | tf_op | source)
XLA Modules:
  0.0 57.7 jit_solution(3267111926192853400)
XLA Ops:
  0.0 0.0 copy-start
  0.0 0.0 copy-start.1
  0.0 0.0 copy-start.2
  0.0 1.8 %gather_rows.1 = (f32[8,8,8,128]{3,2,1,0:T(8,128)S(1)}, f32[8,8,8,128]{3,2,1,0:T(8,128)S(1)}, f32[8,8,8,128]{3,2,1,0:T(8,128)S(1)}, f32[8,8,8,128]{3,2,1,0:T(8,1...) custom-call(s32[64]{0:T(128)} %slot_ref.1, ...), custom_call_target="tpu_custom_call" | custom-call | bytes 4194304 | tf_op jit(solution)/shard_map/gather_rows/pallas_call | solution.py:56
  1.8 2.4 %collective-permute-start.3 = (f32[4,8,8,128]{3,2,1,0:T(8,128)S(1)}, f32[4,8,8,128]{3,2,1,0:T(8,128)S(1)}, u32[]{:S(2)}, u32[]{:S(2)}) collective-permute-start(f32[4,8,8,128]{3,2,1,0:T(8,128)S(1)} %get-tuple-element.21), channel_id=1, source_target_pairs={{0,8},{2,10},{4,12},{6,14},{8,0},{10,2},{12,4},{14,6},{1,9},{3,11}... | collective-permute-start | bytes 393224 | tf_op jit(solution)/shard_map/ppermute | solution.py:269
  4.2 1.2 %collective-permute-start = (f32[8,8,8,128]{3,2,1,0:T(8,128)S(1)}, f32[8,8,8,128]{3,2,1,0:T(8,128)S(1)}, u32[]{:S(2)}, u32[]{:S(2)}) collective-permute-start(f32[8,8,8,128]{3,2,1,0:T(8,128)S(1)} %get-tuple-element.18), channel_id=1, source_target_pairs={{0,2},{2,0},{4,6},{6,4},{8,10},{10,8},{12,14},{14,12},{1,3},{3,1},... | collective-permute-start | bytes 786440 | tf_op jit(solution)/shard_map/ppermute | solution.py:269
  5.5 0.2 collective-permute-start.1
  5.6 1.2 %collective-permute-start.2 = (f32[8,8,8,128]{3,2,1,0:T(8,128)S(1)}, f32[8,8,8,128]{3,2,1,0:T(8,128)S(1)}, u32[]{:S(2)}, u32[]{:S(2)}) collective-permute-start(f32[8,8,8,128]{3,2,1,0:T(8,128)S(1)} %get-tuple-element.20), channel_id=1, source_target_pairs={{0,6},{2,4},{4,2},{6,0},{8,14},{10,12},{12,10},{14,8},{1,7},{3,5},... | collective-permute-start | bytes 786440 | tf_op jit(solution)/shard_map/ppermute | solution.py:269
  6.9 1.0 %collective-permute-start.4 = (f32[8,8,8,128]{3,2,1,0:T(8,128)S(1)}, f32[8,8,8,128]{3,2,1,0:T(8,128)S(1)}, u32[]{:S(2)}, u32[]{:S(2)}) collective-permute-start(f32[8,8,8,128]{3,2,1,0:T(8,128)S(1)} %get-tuple-element.22), channel_id=1, source_target_pairs={{0,10},{2,8},{4,14},{6,12},{8,2},{10,0},{12,6},{14,4},{1,11},{3,9}... | collective-permute-start | bytes 786440 | tf_op jit(solution)/shard_map/ppermute | solution.py:269
  7.9 0.0 copy-done.1
  7.9 0.1 compare_convert_fusion
  8.0 0.0 copy-done
  8.0 0.6 %multiply_reduce_fusion = s32[8,4,8]{2,1,0:T(4,128)S(1)} fusion(s32[64,4,8]{0,2,1:T(8,128)S(1)} %constant_dynamic-slice_fusion, s32[8,64]{1,0:T(8,128)S(1)} %compare_convert_fusion), kind=kLoop, calls=%fused_computation | loop fusion | flops 32512 | bytes 11264 | tf_op jit(solution)/shard_map/reduce_sum | solution.py:247
  8.6 1.6 %collective-permute-done.3.refs_1_ = f32[4,8,8,128]{3,2,1,0:T(8,128)S(1)} collective-permute-done((f32[4,8,8,128]{3,2,1,0:T(8,128)S(1)}, f32[4,8,8,128]{3,2,1,0:T(8,128)S(1)}, u32[]{:S(2)}, u32[]{:S(2)}) %collective-permute-start.3) | collective-permute-done | bytes 131104 | tf_op jit(solution)/shard_map/ppermute | solution.py:269
  10.2 0.0 collective-permute-start.5
  10.2 0.0 copy-done.2
  10.2 0.1 multiply_reduce_fusion.1
  10.3 0.1 copy.13
  10.4 14.7 %collective-permute-done.4.refs_2_.refs_1_ = f32[8,8,8,128]{3,2,1,0:T(8,128)S(1)} collective-permute-done((f32[8,8,8,128]{3,2,1,0:T(8,128)S(1)}, f32[8,8,8,128]{3,2,1,0:T(8,128)S(1)}, u32[]{:S(2)}, u32[]{:S(2)}) %collective-permute-start.4) | collective-permute-done | bytes 262176 | tf_op jit(solution)/shard_map/ppermute | solution.py:269
  25.1 2.7 %collective-permute-start.7 = (f32[4,8,8,128]{3,2,1,0:T(8,128)S(1)}, f32[4,8,8,128]{3,2,1,0:T(8,128)S(1)}, u32[]{:S(2)}, u32[]{:S(2)}) collective-permute-start(f32[4,8,8,128]{3,2,1,0:T(8,128)S(1)} %collective-permute-done.3.refs_1_), channel_id=1, source_target_pairs={{0,1},{1,0},{2,3},{3,2},{4,5},{5,4},{6,7},{7,6},{8,9},{9,8},{10,11... | collective-permute-start | bytes 393224 | tf_op jit(solution)/shard_map/ppermute | solution.py:261
  27.8 0.1 multiply_add_fusion
  27.9 0.1 add.28.bound_ref
  28.0 0.0 collective-permute-done.refs_1_
  28.0 0.1 collective-permute-start.10
  28.1 0.0 collective-permute-done.1.refs_2_
  28.1 0.0 collective-permute-done.2.refs_3_
  28.1 0.2 join_near.1.refs_0_
  28.3 0.1 collective-permute-start.6
  28.3 0.5 collective-permute-start.8
  28.8 6.3 %collective-permute-done.5.refs_3_.refs_1_ = f32[8,8,8,128]{3,2,1,0:T(8,128)S(1)} collective-permute-done((f32[8,8,8,128]{3,2,1,0:T(8,128)S(1)}, f32[8,8,8,128]{3,2,1,0:T(8,128)S(1)}, u32[]{:S(2)}, u32[]{:S(2)}) %collective-permute-start.5) | collective-permute-done | bytes 262176 | tf_op jit(solution)/shard_map/ppermute | solution.py:269
  35.1 9.1 %collective-permute-start.11 = (f32[8,8,8,128]{3,2,1,0:T(8,128)S(1)}, f32[8,8,8,128]{3,2,1,0:T(8,128)S(1)}, u32[]{:S(2)}, u32[]{:S(2)}) collective-permute-start(f32[8,8,8,128]{3,2,1,0:T(8,128)S(1)} %hand_on.5), channel_id=1, source_target_pairs={{0,14},{2,12},{4,10},{6,8},{8,6},{10,4},{12,2},{14,0},{1,15},{3,13... | collective-permute-start | bytes 786440 | tf_op jit(solution)/shard_map/ppermute | solution.py:269
  44.2 0.0 collective-permute-done.7.refs_5_
  44.2 0.9 %collective-permute-start.9 = (f32[8,8,8,128]{3,2,1,0:T(8,128)S(1)}, f32[8,8,8,128]{3,2,1,0:T(8,128)S(1)}, u32[]{:S(2)}, u32[]{:S(2)}) collective-permute-start(f32[8,8,8,128]{3,2,1,0:T(8,128)S(1)} %collective-permute-done.5.refs_3_.refs_1_), channel_id=1, source_target_pairs={{0,1},{1,0},{2,3},{3,2},{4,5},{5,4},{6,7},{7,6},{8,9},{9,8},{10,11... | collective-permute-start | bytes 786440 | tf_op jit(solution)/shard_map/ppermute | solution.py:261
  45.1 6.5 %couple.1.refs_8_.matrix_ref = bf16[8,4,8,64,256]{4,3,2,1,0:T(8,128)(2,1)S(1)} custom-call(s32[256]{0:T(256)S(1)} %add.28.bound_ref, f32[8,4,8,64,128]{4,3,2,1,0:T(8,128)} %factor_ref.1), custom_call_target="tpu_custom_call" | custom-call | flops 30000001024 | bytes 16777216 | tf_op jit(solution)/shard_map/couple/pallas_call | solution.py:168
  51.6 0.0 collective-permute-done.10.refs_0_
  51.6 0.1 collective-permute-start.12
  51.7 0.0 collective-permute-done.11.refs_1_
  51.7 0.5 collective-permute-start.13
  52.2 0.0 collective-permute-done.8.refs_6_
  52.2 0.0 collective-permute-done.9.refs_7_
  52.2 0.0 collective-permute-done.6.refs_4_
  52.2 0.3 lay_rows.1
  52.6 0.5 collective-permute-done.12.refs_2_
  53.1 0.4 collective-permute-done.13.refs_3_
  53.4 4.2 %butterfly.1 = (f32[8,8,64,128]{3,2,1,0:T(8,128)}, f32[8,8,64,128]{3,2,1,0:T(8,128)S(1)}, f32[8,8,64,128]{3,2,1,0:T(8,128)S(1)}) custom-call(bf16[8,4,8,64,256]{4,3,2,1,0:T(8,128)(2,1)S(1)} %couple.1.refs_8_.matrix_ref, f32[8,8,64,128]{3,2,1,0:T(8,128)S(1)} %get-tuple-element.24.own_ref, ...), custom_call_target="tpu_custom_call", output_to_operand_aliasing={{1}: (1, {}), {2}: (2, {})} | custom-call | tf_op jit(solution)/shard_map/butterfly/pallas_call | solution.py:229
  (5 shorter events, 0.0 us)
Async XLA Ops:
  0.0 8.0 %copy-start = (s32[64,4,16]{0,2,1:T(8,128)S(1)}, s32[64,4,16]{0,2,1:T(8,128)}, u32[]{:S(2)}) copy-start(s32[64,4,16]{0,2,1:T(8,128)} %param.9) | copy-start | bytes 49156
  0.0 7.9 %copy-start.1 = (s32[64]{0:T(128)S(1)}, s32[64]{0:T(128)}, u32[]{:S(2)}) copy-start(s32[64]{0:T(128)} %slot_ref.1) | copy-start | bytes 772
  0.0 10.2 %copy-start.2 = (s32[64,4]{0,1:T(4,128)S(1)}, s32[64,4]{0,1:T(4,128)}, u32[]{:S(2)}) copy-start(s32[64,4]{0,1:T(4,128)} %param.8) | copy-start | bytes 3076
  1.8 8.3 %collective-permute-start.3 = (f32[4,8,8,128]{3,2,1,0:T(8,128)S(1)}, f32[4,8,8,128]{3,2,1,0:T(8,128)S(1)}, u32[]{:S(2)}, u32[]{:S(2)}) collective-permute-start(f32[4,8,8,128]{3,2,1,0:T(8,128)S(1)} %get-tuple-element.21), channel_id=1, source_target_pairs={{0,8},{2,10},{4,12},{6,14},{8,0},{10,2},{12,4},{14,6},{1,9},{3,11}... | collective-permute-start | bytes 393224 | tf_op jit(solution)/shard_map/ppermute | solution.py:269
  4.2 23.7 %collective-permute-start = (f32[8,8,8,128]{3,2,1,0:T(8,128)S(1)}, f32[8,8,8,128]{3,2,1,0:T(8,128)S(1)}, u32[]{:S(2)}, u32[]{:S(2)}) collective-permute-start(f32[8,8,8,128]{3,2,1,0:T(8,128)S(1)} %get-tuple-element.18), channel_id=1, source_target_pairs={{0,2},{2,0},{4,6},{6,4},{8,10},{10,8},{12,14},{14,12},{1,3},{3,1},... | collective-permute-start | bytes 786440 | tf_op jit(solution)/shard_map/ppermute | solution.py:269
  5.5 22.6 %collective-permute-start.1 = (f32[8,8,8,128]{3,2,1,0:T(8,128)S(1)}, f32[8,8,8,128]{3,2,1,0:T(8,128)S(1)}, u32[]{:S(2)}, u32[]{:S(2)}) collective-permute-start(f32[8,8,8,128]{3,2,1,0:T(8,128)S(1)} %get-tuple-element.19), channel_id=1, source_target_pairs={{0,4},{2,6},{4,0},{6,2},{8,12},{10,14},{12,8},{14,10},{1,5},{3,7},... | collective-permute-start | bytes 786440 | tf_op jit(solution)/shard_map/ppermute | solution.py:269
  5.6 22.4 %collective-permute-start.2 = (f32[8,8,8,128]{3,2,1,0:T(8,128)S(1)}, f32[8,8,8,128]{3,2,1,0:T(8,128)S(1)}, u32[]{:S(2)}, u32[]{:S(2)}) collective-permute-start(f32[8,8,8,128]{3,2,1,0:T(8,128)S(1)} %get-tuple-element.20), channel_id=1, source_target_pairs={{0,6},{2,4},{4,2},{6,0},{8,14},{10,12},{12,10},{14,8},{1,7},{3,5},... | collective-permute-start | bytes 786440 | tf_op jit(solution)/shard_map/ppermute | solution.py:269
  6.9 18.2 %collective-permute-start.4 = (f32[8,8,8,128]{3,2,1,0:T(8,128)S(1)}, f32[8,8,8,128]{3,2,1,0:T(8,128)S(1)}, u32[]{:S(2)}, u32[]{:S(2)}) collective-permute-start(f32[8,8,8,128]{3,2,1,0:T(8,128)S(1)} %get-tuple-element.22), channel_id=1, source_target_pairs={{0,10},{2,8},{4,14},{6,12},{8,2},{10,0},{12,6},{14,4},{1,11},{3,9}... | collective-permute-start | bytes 786440 | tf_op jit(solution)/shard_map/ppermute | solution.py:269
  10.2 24.9 %collective-permute-start.5 = (f32[8,8,8,128]{3,2,1,0:T(8,128)S(1)}, f32[8,8,8,128]{3,2,1,0:T(8,128)S(1)}, u32[]{:S(2)}, u32[]{:S(2)}) collective-permute-start(f32[8,8,8,128]{3,2,1,0:T(8,128)S(1)} %hand_on.3), channel_id=1, source_target_pairs={{0,12},{2,14},{4,8},{6,10},{8,4},{10,6},{12,0},{14,2},{1,13},{3,15... | collective-permute-start | bytes 786440 | tf_op jit(solution)/shard_map/ppermute | solution.py:269
  25.1 19.1 %collective-permute-start.7 = (f32[4,8,8,128]{3,2,1,0:T(8,128)S(1)}, f32[4,8,8,128]{3,2,1,0:T(8,128)S(1)}, u32[]{:S(2)}, u32[]{:S(2)}) collective-permute-start(f32[4,8,8,128]{3,2,1,0:T(8,128)S(1)} %collective-permute-done.3.refs_1_), channel_id=1, source_target_pairs={{0,1},{1,0},{2,3},{3,2},{4,5},{5,4},{6,7},{7,6},{8,9},{9,8},{10,11... | collective-permute-start | bytes 393224 | tf_op jit(solution)/shard_map/ppermute | solution.py:261
  28.0 23.7 %collective-permute-start.10 = (f32[4,8,8,128]{3,2,1,0:T(8,128)S(1)}, f32[4,8,8,128]{3,2,1,0:T(8,128)S(1)}, u32[]{:S(2)}, u32[]{:S(2)}) collective-permute-start(f32[4,8,8,128]{3,2,1,0:T(8,128)S(1)} %hand_on.4), channel_id=1, source_target_pairs={{0,8},{2,10},{4,12},{6,14},{8,0},{10,2},{12,4},{14,6},{1,9},{3,11}... | collective-permute-start | bytes 393224 | tf_op jit(solution)/shard_map/ppermute | solution.py:269
  28.3 24.0 %collective-permute-start.6 = (f32[8,8,32,128]{3,2,1,0:T(8,128)S(1)}, f32[8,8,32,128]{3,2,1,0:T(8,128)S(1)}, u32[]{:S(2)}, u32[]{:S(2)}) collective-permute-start(f32[8,8,32,128]{3,2,1,0:T(8,128)S(1)} %join_near.1.refs_0_), channel_id=1, source_target_pairs={{0,1},{1,0},{2,3},{3,2},{4,5},{5,4},{6,7},{7,6},{8,9},{9,8},{10,11... | collective-permute-start | bytes 3145736 | tf_op jit(solution)/shard_map/ppermute | solution.py:261
  28.3 23.9 %collective-permute-start.8 = (f32[8,8,8,128]{3,2,1,0:T(8,128)S(1)}, f32[8,8,8,128]{3,2,1,0:T(8,128)S(1)}, u32[]{:S(2)}, u32[]{:S(2)}) collective-permute-start(f32[8,8,8,128]{3,2,1,0:T(8,128)S(1)} %collective-permute-done.4.refs_2_.refs_1_), channel_id=1, source_target_pairs={{0,1},{1,0},{2,3},{3,2},{4,5},{5,4},{6,7},{7,6},{8,9},{9,8},{10,11... | collective-permute-start | bytes 786440 | tf_op jit(solution)/shard_map/ppermute | solution.py:261
  35.1 16.6 %collective-permute-start.11 = (f32[8,8,8,128]{3,2,1,0:T(8,128)S(1)}, f32[8,8,8,128]{3,2,1,0:T(8,128)S(1)}, u32[]{:S(2)}, u32[]{:S(2)}) collective-permute-start(f32[8,8,8,128]{3,2,1,0:T(8,128)S(1)} %hand_on.5), channel_id=1, source_target_pairs={{0,14},{2,12},{4,10},{6,8},{8,6},{10,4},{12,2},{14,0},{1,15},{3,13... | collective-permute-start | bytes 786440 | tf_op jit(solution)/shard_map/ppermute | solution.py:269
  44.2 8.0 %collective-permute-start.9 = (f32[8,8,8,128]{3,2,1,0:T(8,128)S(1)}, f32[8,8,8,128]{3,2,1,0:T(8,128)S(1)}, u32[]{:S(2)}, u32[]{:S(2)}) collective-permute-start(f32[8,8,8,128]{3,2,1,0:T(8,128)S(1)} %collective-permute-done.5.refs_3_.refs_1_), channel_id=1, source_target_pairs={{0,1},{1,0},{2,3},{3,2},{4,5},{5,4},{6,7},{7,6},{8,9},{9,8},{10,11... | collective-permute-start | bytes 786440 | tf_op jit(solution)/shard_map/ppermute | solution.py:261
  51.6 1.4 %collective-permute-start.12 = (f32[4,8,8,128]{3,2,1,0:T(8,128)S(1)}, f32[4,8,8,128]{3,2,1,0:T(8,128)S(1)}, u32[]{:S(2)}, u32[]{:S(2)}) collective-permute-start(f32[4,8,8,128]{3,2,1,0:T(8,128)S(1)} %collective-permute-done.10.refs_0_), channel_id=1, source_target_pairs={{0,1},{1,0},{2,3},{3,2},{4,5},{5,4},{6,7},{7,6},{8,9},{9,8},{10,11... | collective-permute-start | bytes 393224 | tf_op jit(solution)/shard_map/ppermute | solution.py:261
  51.7 1.7 %collective-permute-start.13 = (f32[8,8,8,128]{3,2,1,0:T(8,128)S(1)}, f32[8,8,8,128]{3,2,1,0:T(8,128)S(1)}, u32[]{:S(2)}, u32[]{:S(2)}) collective-permute-start(f32[8,8,8,128]{3,2,1,0:T(8,128)S(1)} %collective-permute-done.11.refs_1_), channel_id=1, source_target_pairs={{0,1},{1,0},{2,3},{3,2},{4,5},{5,4},{6,7},{7,6},{8,9},{9,8},{10,11... | collective-permute-start | bytes 786440 | tf_op jit(solution)/shard_map/ppermute | solution.py:261
